TPU v7x, 32 devices: a whole 2x2x4 slice. The times are simulated.
32 devices in a mesh: dp: 8 (over z, x), tensor: 4 (over y, core).
Axes of the slice: x: 2, y: 2, z: 4, core: 2. Of those that a mesh axis runs over, the one named last changes fastest.
Arguments:
- tokens: bfloat16 [16384, 1024], P(('dp', 'tensor')), may hold values from -6 to 6
- cotangent: bfloat16 [16384, 1024], P(('dp', 'tensor')), may hold values from -6 to 6
- attention_gain: float32 [1024], replicated, may hold values from 0.5 to 1.5
- feedforward_gain: float32 [1024], replicated, may hold values from 0.5 to 1.5
- query_key_value_matrix: bfloat16 [3, 1024, 1024], P(None, 'dp', 'tensor'), may hold values from -0.1875 to 0.1875
- output_matrix: bfloat16 [1024, 1024], P('tensor', 'dp'), may hold values from -0.5 to 0.5
- feedforward_matrix: bfloat16 [2, 1024, 2816], P(None, 'dp', 'tensor'), may hold values from -0.1875 to 0.1875
- down_matrix: bfloat16 [2816, 1024], P('tensor', 'dp'), may hold values from -0.109375 to 0.109375
- memory_retention: float32 [8], replicated, may hold values from 0.3 to 0.98
- memory_step_size: float32 [8], replicated, may hold values from 0.2 to 0.9
- sequence_length: int32 [24], replicated, may hold values from 64 to 1920, as said below
- sequence_permutation: int32 [24], replicated, may hold values from 0 to 23, as said below
- sequence_adapter: int32 [24], replicated, may hold values from 0 to 7
- head_span_window: int32 [8], replicated, may hold values from 256 to 1024, as said below
- query_key_value_lower: bfloat16 [3, 1024, 128], P(None, ('dp', 'tensor')), may hold values from -0.1875 to 0.1875
- query_key_value_upper: bfloat16 [3, 128, 1024], P(None, None, ('dp', 'tensor')), may hold values from -0.75 to 0.75
- output_adapter_lower: bfloat16 [1024, 128], P(('dp', 'tensor')), may hold values from -0.1875 to 0.1875
- output_adapter_upper: bfloat16 [128, 1024], P(None, ('dp', 'tensor')), may hold values from -0.75 to 0.75
- feedforward_adapter_lower: bfloat16 [2, 1024, 128], P(None, ('dp', 'tensor')), may hold values from -0.1875 to 0.1875
- feedforward_adapter_upper: bfloat16 [2, 128, 2816], P(None, None, ('dp', 'tensor')), may hold values from -0.75 to 0.75
- down_adapter_lower: bfloat16 [2816, 128], P(('dp', 'tensor')), may hold values from -0.109375 to 0.109375
- down_adapter_upper: bfloat16 [128, 1024], P(None, ('dp', 'tensor')), may hold values from -0.75 to 0.75
Outputs:
- mixed: bfloat16 [16384, 1024], P(('dp', 'tensor'))
- token_grad: bfloat16 [16384, 1024], P(('dp', 'tensor'))
- qkv_lora_a_grad: float32 [3, 1024, 128], P(None, ('dp', 'tensor'))
- qkv_lora_b_grad: float32 [3, 128, 1024], P(None, None, ('dp', 'tensor'))
- out_lora_a_grad: float32 [1024, 128], P(('dp', 'tensor'))
- out_lora_b_grad: float32 [128, 1024], P(None, ('dp', 'tensor'))
- ffn_lora_a_grad: float32 [2, 1024, 128], P(None, ('dp', 'tensor'))
- ffn_lora_b_grad: float32 [2, 128, 2816], P(None, None, ('dp', 'tensor'))
- down_lora_a_grad: float32 [2816, 128], P(('dp', 'tensor'))
- down_lora_b_grad: float32 [128, 1024], P(None, ('dp', 'tensor'))
Inputs may be any that keep to these rules, and one draw needn't show every extreme that they name: `sequence_length`: multiples of 64; the 3 sequences that sequence_permutation lists for a group sum to 2048. `sequence_permutation`: a permutation of the sequence numbers. `head_span_window`: multiples of 256.
All inputs are finite; a program needn't handle non-finite values.
Results may differ from a plain program's by a relative error of at most 0.02.
Values may be sent and summed in bfloat16 or wider, within the bound.
No kernel may reach another device: no remote copies, remote signals or barrier semaphores. Data moves between devices by JAX's collectives and lax.ppermute only.
A program may use at most 192 MiB of HBM per device.

v0:
```python
import jax
import jax.numpy as jnp
from jax import lax
from jax.sharding import PartitionSpec as P

HEAD_DIM = 128
ADAPTER_RANK = 16
STRETCH = 64
WIN_MAX = 1024
QBLK = 512
SEQ_G = 3
ADAPTER_COLUMNS = 128


highest = lax.Precision.HIGHEST
memory_gain = 32.0
epsilon = 1e-06


def normalize(values, gain):
    return values * lax.rsqrt(jnp.mean(values * values, -1, keepdims=True) + epsilon) * gain


def pick_rows(lookup, wanted):
    hits = wanted[:, None] == jnp.arange(lookup.shape[0], dtype=jnp.int32)[None, :]
    return jnp.sum(jnp.where(hits, lookup[None, :], 0), 1)


def stream_layout(sequence_length, sequence_permutation, sequence_adapter, group_number, row_count):
    members = lax.dynamic_slice_in_dim(sequence_permutation, group_number * SEQ_G, SEQ_G)
    member_length = pick_rows(sequence_length, members)
    member_adapter = pick_rows(sequence_adapter, members)
    begins = jnp.cumsum(member_length) - member_length
    positions = jnp.arange(row_count, dtype=jnp.int32)
    seq_index = jnp.sum((positions[:, None] >= begins[None, :]).astype(jnp.int32), 1) - 1
    return (seq_index, pick_rows(member_adapter, seq_index), pick_rows(begins, seq_index))


def adapter_mask(row_adapter):
    column_count = jnp.arange(ADAPTER_COLUMNS, dtype=jnp.int32)[None, :] // ADAPTER_RANK
    return (column_count == row_adapter[:, None]).astype(jnp.float32)


def memory_read(queries, key_heads, value_heads, decay_own, rate_own, stretch_first):
    row_count, head_count, head_dim = queries.shape
    query_unit = queries * lax.rsqrt(jnp.sum(queries * queries, -1, keepdims=True) + epsilon)
    key_unit = key_heads * lax.rsqrt(jnp.sum(key_heads * key_heads, -1, keepdims=True) + epsilon)
    stretches = row_count // STRETCH
    shaped = (stretches, STRETCH, head_count, head_dim)

    def advance(memory_state, input_rows):
        query_stretch, key_stretch, value_stretch, reset_flag = input_rows
        memory_state = jnp.where(reset_flag, jnp.zeros_like(memory_state), memory_state)
        read_out = jnp.einsum("thd,hde->the", query_stretch, memory_state, precision=highest)
        error_rows = (
            jnp.einsum("thd,hde->the", key_stretch, memory_state, precision=highest) - value_stretch
        )
        update = jnp.einsum("thd,the->hde", key_stretch, error_rows, precision=highest) / STRETCH
        memory_state = decay_own[:, None, None] * memory_state - rate_own[:, None, None] * update
        return (memory_state, read_out)

    initial = jnp.zeros((head_count, head_dim, head_dim), jnp.float32)
    final_state, reads = lax.scan(
        jax.checkpoint(advance),
        initial,
        (
            query_unit.reshape(shaped),
            key_unit.reshape(shaped),
            value_heads.reshape(shaped),
            stretch_first,
        ),
    )
    return reads.reshape(row_count, head_count, head_dim)


def block_parts(queries, padded_keys, padded_values, seq_index, padded_seq, windows, number):
    key_span = QBLK + WIN_MAX
    first_row = number * QBLK
    query_block = lax.dynamic_slice_in_dim(queries, first_row, QBLK, 0)
    key_block = lax.dynamic_slice_in_dim(padded_keys, first_row, key_span, 0)
    value_block = lax.dynamic_slice_in_dim(padded_values, first_row, key_span, 0)
    distance = (
        jnp.arange(QBLK, dtype=jnp.int32)[:, None]
        + WIN_MAX
        - jnp.arange(key_span, dtype=jnp.int32)[None, :]
    )
    same_seq = (
        lax.dynamic_slice_in_dim(seq_index, first_row, QBLK)[:, None]
        == lax.dynamic_slice_in_dim(padded_seq, first_row, key_span)[None, :]
    )
    allowed = (distance >= 0)[None] & (distance[None] < windows[:, None, None]) & same_seq[None]
    score_scale = queries.shape[2] ** (-0.5)
    scores = (
        jnp.einsum("qhd,khd->hqk", query_block, key_block, preferred_element_type=jnp.float32)
        * score_scale
    )
    return (query_block, key_block, value_block, jnp.where(allowed, scores, -1e30))


def padded_inputs(key_heads, value_heads, seq_index):
    padded_keys = jnp.pad(key_heads, ((WIN_MAX, 0), (0, 0), (0, 0)))
    padded_values = jnp.pad(value_heads, ((WIN_MAX, 0), (0, 0), (0, 0)))
    padded_seq = jnp.pad(seq_index, (WIN_MAX, 0), constant_values=-1)
    return (padded_keys, padded_values, padded_seq)


def attend_forward(queries, key_heads, value_heads, seq_index, windows):
    row_count, head_count, head_dim = queries.shape
    padded_keys, padded_values, padded_seq = padded_inputs(key_heads, value_heads, seq_index)

    def block_out(number):
        query_block, key_block, value_block, scores = block_parts(
            queries, padded_keys, padded_values, seq_index, padded_seq, windows, number
        )
        row_max = jnp.max(scores, -1, keepdims=True)
        exponent = jnp.exp(scores - row_max)
        row_total = jnp.sum(exponent, -1, keepdims=True)
        soft_weights = (exponent / row_total).astype(jnp.bfloat16)
        attended = jnp.einsum(
            "hqk,khd->qhd", soft_weights, value_block, preferred_element_type=jnp.float32
        )
        return (attended, row_max + jnp.log(row_total))

    outputs, log_totals = lax.map(block_out, jnp.arange(row_count // QBLK, dtype=jnp.int32))
    return (outputs.reshape(row_count, head_count, head_dim), log_totals)


def attend_backward(queries, key_heads, value_heads, seq_index, windows, log_totals, grad_heads):
    row_count, head_count, head_dim = queries.shape
    score_scale = head_dim ** (-0.5)
    key_span = QBLK + WIN_MAX
    padded_keys, padded_values, padded_seq = padded_inputs(key_heads, value_heads, seq_index)

    def accumulate(number, carried):
        grad_query, grad_key, grad_value = carried
        query_block, key_block, value_block, scores = block_parts(
            queries, padded_keys, padded_values, seq_index, padded_seq, windows, number
        )
        first_row = number * QBLK
        soft_weights = jnp.exp(scores - log_totals[number])
        grad_block = lax.dynamic_slice_in_dim(grad_heads, first_row, QBLK, 0)
        grad_soft = jnp.einsum(
            "qhd,khd->hqk", grad_block, value_block, preferred_element_type=jnp.float32
        )
        inner_sum = jnp.sum(soft_weights * grad_soft, -1, keepdims=True)
        grad_scores = (soft_weights * (grad_soft - inner_sum)).astype(jnp.bfloat16)
        block_query = (
            jnp.einsum("hqk,khd->qhd", grad_scores, key_block, preferred_element_type=jnp.float32)
            * score_scale
        )
        block_key = (
            jnp.einsum("hqk,qhd->khd", grad_scores, query_block, preferred_element_type=jnp.float32)
            * score_scale
        )
        block_value = jnp.einsum(
            "hqk,qhd->khd",
            soft_weights.astype(jnp.bfloat16),
            grad_block,
            preferred_element_type=jnp.float32,
        )
        grad_query = lax.dynamic_update_slice_in_dim(grad_query, block_query, first_row, 0)
        grad_key = lax.dynamic_update_slice_in_dim(
            grad_key,
            lax.dynamic_slice_in_dim(grad_key, first_row, key_span, 0) + block_key,
            first_row,
            0,
        )
        grad_value = lax.dynamic_update_slice_in_dim(
            grad_value,
            lax.dynamic_slice_in_dim(grad_value, first_row, key_span, 0) + block_value,
            first_row,
            0,
        )
        return (grad_query, grad_key, grad_value)

    padded_shape = (row_count + WIN_MAX, head_count, head_dim)
    initial = (
        jnp.zeros(queries.shape, jnp.float32),
        jnp.zeros(padded_shape, jnp.float32),
        jnp.zeros(padded_shape, jnp.float32),
    )
    results = lax.fori_loop(0, row_count // QBLK, accumulate, initial)
    return (results[0], results[1][WIN_MAX:], results[2][WIN_MAX:])


def gather_stream(values):
    return lax.all_gather(values, "tensor", axis=0, tiled=True)


def input_grads(row_term, quarter):
    return lax.psum_scatter(
        row_term(jnp.int32(0), quarter * lax.axis_size("tensor")).astype(jnp.bfloat16),
        "tensor",
        scatter_dimension=0,
        tiled=True,
    ).astype(jnp.float32)


def projection_inward(
    input_rows, weight_locals, adapter_lower, adapter_upper_local, expand_columns
):
    outputs = []
    latents = []
    for member_sequence in range(weight_locals.shape[0]):
        latent_value = (
            expand_columns
            * jnp.dot(
                input_rows, adapter_lower[member_sequence], preferred_element_type=jnp.float32
            )
        ).astype(jnp.bfloat16)
        outputs.append(
            jnp.dot(input_rows, weight_locals[member_sequence], preferred_element_type=jnp.float32)
            + jnp.dot(
                latent_value,
                adapter_upper_local[member_sequence],
                preferred_element_type=jnp.float32,
            )
        )
        latents.append(latent_value)
    return (outputs, latents)


def back_in(
    input_rows,
    gradient_list,
    weight_locals,
    adapter_lower,
    adapter_upper_local,
    latents,
    expand_columns,
    quarter,
    portion_index,
    portion_count,
):
    count_in = len(gradient_list)
    d_latents = [
        (
            expand_columns
            * jnp.dot(
                gradient_list[member_sequence],
                adapter_upper_local[member_sequence].T,
                preferred_element_type=jnp.float32,
            )
        ).astype(jnp.bfloat16)
        for member_sequence in range(count_in)
    ]

    def row_term(first_row, row_total):
        summed = jnp.zeros((row_total, input_rows.shape[1]), jnp.float32)
        for member_sequence in range(count_in):
            gradient_rows = gradient_list[member_sequence]
            latent_row_block = d_latents[member_sequence]
            summed = summed + jnp.dot(
                gradient_rows, weight_locals[member_sequence].T, preferred_element_type=jnp.float32
            )
            summed = summed + jnp.dot(
                latent_row_block,
                adapter_lower[member_sequence].T,
                preferred_element_type=jnp.float32,
            )
        return summed

    grad_inputs = input_grads(row_term, quarter)
    a_terms = jnp.stack(
        [
            jnp.dot(input_rows.T, d_latents[member_sequence], preferred_element_type=jnp.float32)
            for member_sequence in range(count_in)
        ]
    )
    b_own = jnp.stack(
        [
            jnp.dot(
                latents[member_sequence].T,
                gradient_list[member_sequence],
                preferred_element_type=jnp.float32,
            )
            for member_sequence in range(count_in)
        ]
    )
    local_width = b_own.shape[2]
    b_terms = lax.dynamic_update_slice_in_dim(
        jnp.zeros((count_in, b_own.shape[1], local_width * portion_count), jnp.float32),
        b_own,
        portion_index * local_width,
        2,
    )
    return (grad_inputs, a_terms, b_terms)


def projection_outward(
    activation_value,
    weight_local,
    adapter_lower_local,
    adapter_upper,
    expand_columns,
    portion_count,
):
    row_count = activation_value.shape[0]
    quarter = row_count // portion_count
    latent_value = (
        expand_columns
        * jnp.dot(activation_value, adapter_lower_local, preferred_element_type=jnp.float32)
    ).astype(jnp.bfloat16)

    def row_term(first_row, row_total):
        return jnp.dot(
            activation_value, weight_local, preferred_element_type=jnp.float32
        ) + jnp.dot(latent_value, adapter_upper, preferred_element_type=jnp.float32)

    result = lax.psum_scatter(
        row_term(jnp.int32(0), quarter * lax.axis_size("tensor")).astype(jnp.bfloat16),
        "tensor",
        scatter_dimension=0,
        tiled=True,
    ).astype(jnp.float32)
    return (result, (activation_value, latent_value))


def project_back(
    gradient_quarter,
    kept_values,
    weight_local,
    adapter_lower_local,
    adapter_upper,
    expand_columns,
    portion_index,
    portion_count,
):
    adapter_width = adapter_upper.shape[0]
    activation_value, latent_value = kept_values
    gradient_rows = lax.all_gather(
        gradient_quarter.astype(jnp.bfloat16), "tensor", axis=0, tiled=True
    )
    latent_gradient = (
        expand_columns * jnp.dot(gradient_rows, adapter_upper.T, preferred_element_type=jnp.float32)
    ).astype(jnp.bfloat16)
    d_activation = jnp.dot(
        gradient_rows, weight_local.T, preferred_element_type=jnp.float32
    ) + jnp.dot(latent_gradient, adapter_lower_local.T, preferred_element_type=jnp.float32)
    b_term = jnp.dot(latent_value.T, gradient_rows, preferred_element_type=jnp.float32)
    a_own = jnp.dot(activation_value.T, latent_gradient, preferred_element_type=jnp.float32)
    local_width = a_own.shape[0]
    a_term = lax.dynamic_update_slice_in_dim(
        jnp.zeros((local_width * portion_count, adapter_width), jnp.float32),
        a_own,
        portion_index * local_width,
        0,
    )
    return (d_activation, a_term, b_term)


def per_device(
    tokens,
    cotangent,
    attention_gain,
    feedforward_gain,
    query_key_value_matrix,
    output_matrix,
    feedforward_matrix,
    down_matrix,
    memory_retention,
    memory_step_size,
    sequence_length,
    sequence_permutation,
    sequence_adapter,
    head_span_window,
    query_key_value_lower,
    query_key_value_upper,
    output_adapter_lower,
    output_adapter_upper,
    feedforward_adapter_lower,
    feedforward_adapter_upper,
    down_adapter_lower,
    down_adapter_upper,
):
    groups_count = lax.axis_size("dp")
    portion_count = lax.axis_size("tensor")
    portion_index = lax.axis_index("tensor")
    group_index = lax.axis_index("dp")
    quarter, width = tokens.shape
    slot_rows = quarter // groups_count
    row_count = quarter * portion_count
    arrived_tokens, arrived_grads = (
        lax.all_to_all(
            tokens.reshape(groups_count, slot_rows, width),
            "dp",
            split_axis=0,
            concat_axis=0,
            tiled=True,
        ),
        lax.all_to_all(
            cotangent.reshape(groups_count, slot_rows, width),
            "dp",
            split_axis=0,
            concat_axis=0,
            tiled=True,
        ),
    )
    stream_in = arrived_tokens.reshape(quarter, width).astype(jnp.float32)
    grad_out = arrived_grads.reshape(quarter, width).astype(jnp.float32)
    qkv_local, out_local, ffn_local, down_local = (
        lax.all_gather(query_key_value_matrix, "dp", axis=1, tiled=True),
        lax.all_gather(output_matrix, "dp", axis=1, tiled=True),
        lax.all_gather(feedforward_matrix, "dp", axis=1, tiled=True),
        lax.all_gather(down_matrix, "dp", axis=1, tiled=True),
    )
    qkv_a, qkv_b, out_a, out_b, ffn_a, ffn_b, down_a, down_b = (
        lax.all_gather(query_key_value_lower, ("dp", "tensor"), axis=1, tiled=True),
        lax.all_gather(query_key_value_upper, ("dp", "tensor"), axis=2, tiled=True),
        lax.all_gather(output_adapter_lower, ("dp", "tensor"), axis=0, tiled=True),
        lax.all_gather(output_adapter_upper, ("dp", "tensor"), axis=1, tiled=True),
        lax.all_gather(feedforward_adapter_lower, ("dp", "tensor"), axis=1, tiled=True),
        lax.all_gather(feedforward_adapter_upper, ("dp", "tensor"), axis=2, tiled=True),
        lax.all_gather(down_adapter_lower, ("dp", "tensor"), axis=0, tiled=True),
        lax.all_gather(down_adapter_upper, ("dp", "tensor"), axis=1, tiled=True),
    )
    head_width = width // portion_count
    hidden_width = ffn_local.shape[2]
    head_local = head_width // HEAD_DIM
    qkv_b_own = lax.dynamic_slice_in_dim(qkv_b, portion_index * head_width, head_width, 2)
    out_a_own = lax.dynamic_slice_in_dim(out_a, portion_index * head_width, head_width, 0)
    ffn_b_own = lax.dynamic_slice_in_dim(ffn_b, portion_index * hidden_width, hidden_width, 2)
    down_a_own = lax.dynamic_slice_in_dim(down_a, portion_index * hidden_width, hidden_width, 0)
    windows = lax.dynamic_slice_in_dim(head_span_window, portion_index * head_local, head_local, 0)
    decay_own = lax.dynamic_slice_in_dim(
        memory_retention, portion_index * head_local, head_local, 0
    )
    rate_own = lax.dynamic_slice_in_dim(memory_step_size, portion_index * head_local, head_local, 0)
    seq_index, row_adapter, row_begin = stream_layout(
        sequence_length, sequence_permutation, sequence_adapter, group_index, row_count
    )
    expand_columns = adapter_mask(row_adapter)
    stretch_first = (
        row_begin.reshape(-1, STRETCH)[:, 0]
        == jnp.arange(row_count // STRETCH, dtype=jnp.int32) * STRETCH
    )
    normed = gather_stream(normalize(stream_in, attention_gain).astype(jnp.bfloat16))
    projected, qkv_latents = projection_inward(normed, qkv_local, qkv_a, qkv_b_own, expand_columns)
    query_heads, key_heads, value_heads = [
        item.astype(jnp.bfloat16).reshape(row_count, head_local, HEAD_DIM) for item in projected
    ]
    attended, log_totals = attend_forward(query_heads, key_heads, value_heads, seq_index, windows)

    def memory_part(query_float, key_float, value_float):
        return memory_read(query_float, key_float, value_float, decay_own, rate_own, stretch_first)

    remembered, memory_pull = jax.vjp(
        memory_part,
        query_heads.astype(jnp.float32),
        key_heads.astype(jnp.float32),
        value_heads.astype(jnp.float32),
    )
    heads_out = (
        (attended + memory_gain * remembered).reshape(row_count, head_width).astype(jnp.bfloat16)
    )
    attn_branch, out_kept = projection_outward(
        heads_out, out_local, out_a_own, out_b, expand_columns, portion_count
    )
    hidden_one = stream_in + attn_branch
    normed_two = gather_stream(normalize(hidden_one, feedforward_gain).astype(jnp.bfloat16))
    ffn_pre, ffn_latents = projection_inward(
        normed_two, ffn_local, ffn_a, ffn_b_own, expand_columns
    )

    def swiglu_part(gate_pre, up_pre):
        return jax.nn.silu(gate_pre) * up_pre

    swiglu_out, swiglu_pull = jax.vjp(swiglu_part, ffn_pre[0], ffn_pre[1])
    ffn_branch, down_kept = projection_outward(
        swiglu_out.astype(jnp.bfloat16),
        down_local,
        down_a_own,
        down_b,
        expand_columns,
        portion_count,
    )
    mixed_rows = (hidden_one + ffn_branch).astype(jnp.bfloat16)
    grad_swiglu, down_a_term, down_b_term = project_back(
        grad_out,
        down_kept,
        down_local,
        down_a_own,
        down_b,
        expand_columns,
        portion_index,
        portion_count,
    )
    grad_gate, grad_up = swiglu_pull(grad_swiglu)
    ffn_grad_list = [grad_gate.astype(jnp.bfloat16), grad_up.astype(jnp.bfloat16)]
    grad_normed_two, ffn_a_term, ffn_b_term = back_in(
        normed_two,
        ffn_grad_list,
        ffn_local,
        ffn_a,
        ffn_b_own,
        ffn_latents,
        expand_columns,
        quarter,
        portion_index,
        portion_count,
    )
    norm_value, norm_pull = jax.vjp(lambda values: normalize(values, feedforward_gain), hidden_one)
    grad_one = grad_out + norm_pull(grad_normed_two)[0]
    grad_heads, out_a_term, out_b_term = project_back(
        grad_one,
        out_kept,
        out_local,
        out_a_own,
        out_b,
        expand_columns,
        portion_index,
        portion_count,
    )
    grad_heads_low = grad_heads.astype(jnp.bfloat16).reshape(row_count, head_local, HEAD_DIM)
    memory_query, memory_key, memory_value = memory_pull(
        memory_gain * grad_heads_low.astype(jnp.float32)
    )
    attn_query, attn_key, attn_value = attend_backward(
        query_heads, key_heads, value_heads, seq_index, windows, log_totals, grad_heads_low
    )
    qkv_grad_list = [
        (attn_query + memory_query).reshape(row_count, head_width).astype(jnp.bfloat16),
        (attn_key + memory_key).reshape(row_count, head_width).astype(jnp.bfloat16),
        (attn_value + memory_value).reshape(row_count, head_width).astype(jnp.bfloat16),
    ]
    grad_normed, qkv_a_term, qkv_b_term = back_in(
        normed,
        qkv_grad_list,
        qkv_local,
        qkv_a,
        qkv_b_own,
        qkv_latents,
        expand_columns,
        quarter,
        portion_index,
        portion_count,
    )
    first_value, first_pull = jax.vjp(lambda values: normalize(values, attention_gain), stream_in)
    grad_input = (grad_one + first_pull(grad_normed)[0]).astype(jnp.bfloat16)
    mixed_back, grad_back = (
        lax.all_to_all(
            mixed_rows.reshape(groups_count, slot_rows, width),
            "dp",
            split_axis=0,
            concat_axis=0,
            tiled=True,
        ),
        lax.all_to_all(
            grad_input.reshape(groups_count, slot_rows, width),
            "dp",
            split_axis=0,
            concat_axis=0,
            tiled=True,
        ),
    )
    summed = (
        lax.psum_scatter(qkv_a_term, ("dp", "tensor"), scatter_dimension=1, tiled=True),
        lax.psum_scatter(qkv_b_term, ("dp", "tensor"), scatter_dimension=2, tiled=True),
        lax.psum_scatter(out_a_term, ("dp", "tensor"), scatter_dimension=0, tiled=True),
        lax.psum_scatter(out_b_term, ("dp", "tensor"), scatter_dimension=1, tiled=True),
        lax.psum_scatter(ffn_a_term, ("dp", "tensor"), scatter_dimension=1, tiled=True),
        lax.psum_scatter(ffn_b_term, ("dp", "tensor"), scatter_dimension=2, tiled=True),
        lax.psum_scatter(down_a_term, ("dp", "tensor"), scatter_dimension=0, tiled=True),
        lax.psum_scatter(down_b_term, ("dp", "tensor"), scatter_dimension=1, tiled=True),
    )
    return (
        mixed_back.reshape(quarter, width),
        grad_back.reshape(quarter, width),
        summed[0],
        summed[1],
        summed[2],
        summed[3],
        summed[4],
        summed[5],
        summed[6],
        summed[7],
    )


def solution(mesh):
    placed = (
        P(("dp", "tensor"), None),
        P(("dp", "tensor"), None),
        P(),
        P(),
        P(None, "dp", "tensor"),
        P("tensor", "dp"),
        P(None, "dp", "tensor"),
        P("tensor", "dp"),
        P(),
        P(),
        P(),
        P(),
        P(),
        P(),
        P(None, ("dp", "tensor"), None),
        P(None, None, ("dp", "tensor")),
        P(("dp", "tensor"), None),
        P(None, ("dp", "tensor")),
        P(None, ("dp", "tensor"), None),
        P(None, None, ("dp", "tensor")),
        P(("dp", "tensor"), None),
        P(None, ("dp", "tensor")),
    )
    return jax.shard_map(
        per_device,
        mesh=mesh,
        in_specs=placed,
        out_specs=(
            P(("dp", "tensor"), None),
            P(("dp", "tensor"), None),
            P(None, ("dp", "tensor"), None),
            P(None, None, ("dp", "tensor")),
            P(("dp", "tensor"), None),
            P(None, ("dp", "tensor")),
            P(None, ("dp", "tensor"), None),
            P(None, None, ("dp", "tensor")),
            P(("dp", "tensor"), None),
            P(None, ("dp", "tensor")),
        ),
        check_vma=False,
    )
```

profile of v0, /device:TPU:2, one launch (start us, length us, event | category | flops | bytes accessed | tf_op | source)
XLA Modules:
  0.0 2794.2 jit_solution(6629283550469927905)
XLA Ops:
  8.0 37.9 %all_to_all.20 = bf16[8,64,1024]{2,1,0:T(8,128)(2,1)S(1)} all-to-all(bf16[8,64,1024]{2,1,0:T(8,128)(2,1)} %bitcast.444), channel_id=1, replica_groups=mesh['dp'=8,'tensor'=4] {'dp'}, dimensions={0} | all-to-all | bytes 2097152 | tf_op jit(solution)/shard_map/all_to_all | solution.py:384
  49.9 40.0 %all_gather.53 = bf16[1024,128]{1,0:T(8,128)(2,1)} all-gather(bf16[32,128]{1,0:T(8,128)(2,1)S(1)} %copy-done.89), channel_id=1, replica_groups=mesh['dp'=8,'tensor'=4] {'dp','tensor'}, dimensions={0}, use_global_device_ids=true | all-gather | bytes 270336 | tf_op jit(solution)/shard_map/all_gather | solution.py:410
  90.0 37.3 %all_gather.54 = bf16[128,1024]{0,1:T(8,128)(2,1)S(1)} all-gather(bf16[128,32]{0,1:T(8,128)(2,1)S(1)} %copy-done.90), channel_id=1, replica_groups=mesh['dp'=8,'tensor'=4] {'dp','tensor'}, dimensions={1}, use_global_device_ids=true | all-gather | bytes 270336 | tf_op jit(solution)/shard_map/all_gather | solution.py:411
  127.8 29.8 %all_gather.52 = bf16[256,1024]{1,0:T(8,128)(2,1)} all-gather(bf16[256,128]{1,0:T(8,128)(2,1)S(1)} %copy-done.73), channel_id=1, replica_groups=mesh['dp'=8,'tensor'=4] {'dp'}, dimensions={1}, use_global_device_ids=true | all-gather | bytes 589824 | tf_op jit(solution)/shard_map/all_gather | solution.py:403
  157.6 39.0 %all_gather.50 = bf16[3,1024,128]{2,1,0:T(8,128)(2,1)S(1)} all-gather(bf16[3,32,128]{2,1,0:T(8,128)(2,1)S(1)} %copy-done.78), channel_id=1, replica_groups=mesh['dp'=8,'tensor'=4] {'dp','tensor'}, dimensions={1}, use_global_device_ids=true | all-gather | bytes 811008 | tf_op jit(solution)/shard_map/all_gather | solution.py:408
  196.7 41.6 %all_gather.51 = bf16[3,128,1024]{1,2,0:T(8,128)(2,1)} all-gather(bf16[3,128,32]{1,2,0:T(8,128)(2,1)S(1)} %copy-done.79), channel_id=1, replica_groups=mesh['dp'=8,'tensor'=4] {'dp','tensor'}, dimensions={2}, use_global_device_ids=true | all-gather | bytes 811008 | tf_op jit(solution)/shard_map/all_gather | solution.py:409
  275.0 4.1 broadcast_multiply_fusion.1
  289.1 4.5 reshape.461
  293.7 5.0 copy.179
  300.3 233.1 %while.67 = (s32[]{:T(128)}, f32[2,128,128]{2,1,0:T(8,128)S(1)}, f32[32,64,2,128]{3,1,2,0:T(8,128)}, f32[32,2,128,128]{3,2,1,0:T(8,128)}, f32[2,1,1]{0,2,1:T(1,1...) while((s32[]{:T(128)}, f32[2,128,128]{2,1,0:T(8,128)S(1)}, ...), condition=%wide.region_14.15_spmd.clone, body=%wide.region_13.14_spmd.clone.sunk | while | flops 75841536 | bytes 1249960 | solution.py:63
  542.5 50.3 %while.65 = (s32[]{:T(128)}, f32[4,512,2,128]{3,2,1,0:T(2,128)}, f32[4,2,512,1]{2,1,3,0:T(2,128)}, s32[4]{0:T(128)S(1)}, bf16[3072,2,128]{2,0,1:T(8,128)(2,1)}, ...) while((s32[]{:T(128)}, f32[4,512,2,128]{3,2,1,0:T(2,128)}, ...), condition=%wide.region_9.10_spmd, body=%wide.region_6.9_spmd.sunk | while | flops 825753088 | bytes 32833268 | solution.py:124
  603.2 33.2 %all_to_all.21 = bf16[8,64,1024]{2,1,0:T(8,128)(2,1)} all-to-all(bf16[8,64,1024]{2,1,0:T(8,128)(2,1)S(1)} %bitcast.445), channel_id=1, replica_groups=mesh['dp'=8,'tensor'=4] {'dp'}, dimensions={0} | all-to-all | bytes 2097152 | tf_op jit(solution)/shard_map/all_to_all | solution.py:391
  636.5 11.3 reduce-scatter.16.cloned.1.call-done
  652.6 42.2 %all_gather.57 = bf16[2,1024,128]{2,1,0:T(8,128)(2,1)} all-gather(bf16[2,32,128]{2,1,0:T(8,128)(2,1)S(1)} %copy-done.87), channel_id=1, replica_groups=mesh['dp'=8,'tensor'=4] {'dp','tensor'}, dimensions={1}, use_global_device_ids=true | all-gather | bytes 540672 | tf_op jit(solution)/shard_map/all_gather | solution.py:412
  694.7 40.7 %all_gather.61 = bf16[128,1024]{0,1:T(8,128)(2,1)} all-gather(bf16[128,32]{0,1:T(8,128)(2,1)S(1)} %copy-done.91), channel_id=1, replica_groups=mesh['dp'=8,'tensor'=4] {'dp','tensor'}, dimensions={1}, use_global_device_ids=true | all-gather | bytes 270336 | tf_op jit(solution)/shard_map/all_gather | solution.py:415
  735.4 43.1 %all_gather.60 = bf16[2816,128]{1,0:T(8,128)(2,1)} all-gather(bf16[88,128]{1,0:T(8,128)(2,1)S(1)} %copy-done.80), channel_id=1, replica_groups=mesh['dp'=8,'tensor'=4] {'dp','tensor'}, dimensions={0}, use_global_device_ids=true | all-gather | bytes 743424 | tf_op jit(solution)/shard_map/all_gather | solution.py:414
  778.6 5.6 fusion.154
  786.2 4.3 convolution_add_fusion.2
  790.6 4.4 fusion.91
  797.1 39.1 %all-gather.15.cloned.1.call-done = bf16[2,1024,704]{1,2,0:T(8,128)(2,1)} async-done(((bf16[2,128,704]{1,2,0:T(8,128)(2,1)}), bf16[2,1024,704]{1,2,0:T(8,128)(2,1)}) %all-gather.15.cloned.1.call-update) | async-done | bytes 2883600 | tf_op jit(solution)/shard_map/all_gather | solution.py:404
  836.2 8.5 fusion.121
  844.6 5.0 fusion.119
  849.6 42.8 %all-gather.17.cloned.1.call-done = bf16[2,128,2816]{1,2,0:T(8,128)(2,1)} async-done(((bf16[2,128,88]{1,2,0:T(8,128)(2,1)}), bf16[2,128,2816]{1,2,0:T(8,128)(2,1)}) %all-gather.17.cloned.1.call-update) | async-done | bytes 1441808 | tf_op jit(solution)/shard_map/all_gather | solution.py:413
  897.1 7.4 fusion.81
  908.9 5.9 fusion.118
  917.0 5.8 fusion.120
  922.8 9.6 add_convert_fusion.1
  932.4 43.6 %reduce-scatter.20.cloned.1.call-done = bf16[512,1024]{1,0:T(8,128)(2,1)} async-done(((bf16[2048,1024]{1,0:T(8,128)(2,1)}), bf16[512,1024]{1,0:T(8,128)(2,1)}) %reduce-scatter.20.cloned.1.call-update) | async-done | bytes 1048592 | tf_op jit(solution)/shard_map/reduce_scatter | solution.py:191
  980.8 33.7 %all-gather.23.cloned.1.call-done = bf16[2048,1024]{1,0:T(8,128)(2,1)} async-done(((bf16[512,1024]{1,0:T(8,128)(2,1)}), bf16[2048,1024]{1,0:T(8,128)(2,1)}) %all-gather.23.cloned.1.call-update) | async-done | bytes 4194320 | tf_op jit(solution)/shard_map/all_gather | solution.py:331
  1024.9 4.6 copy.188
  1034.4 315.6 %while.68 = (s32[]{:T(128)}, f32[2,128,128]{2,1,0:T(8,128)S(1)}, f32[32,64,2,128]{3,1,2,0:T(8,128)}, f32[32,64,2,128]{3,1,2,0:T(8,128)}, f32[32,64,2,128]{3,1,0,...) while((s32[]{:T(128)}, f32[2,128,128]{2,1,0:T(8,128)S(1)}, ...), condition=%wide.region_24.25_spmd.clone, body=%wide.region_23.24_spmd.clone.sunk | while | flops 176668672 | bytes 3343587 | solution.py:63
  1353.4 12.0 fusion.116
  1372.6 191.3 %while.66 = (s32[]{:T(128)}, f32[2048,2,128]{2,0,1:T(8,128)}, f32[3072,2,128]{2,0,1:T(8,128)}, f32[3072,2,128]{2,0,1:T(8,128)}, bf16[3072,2,128]{2,0,1:T(8,128)(...) while((s32[]{:T(128)}, f32[2048,2,128]{2,0,1:T(8,128)}, ...), condition=%wide.region_22.23_spmd, body=%wide.region_20.22_spmd.sunk | while | flops 2036596224 | bytes 127716200 | solution.py:182
  1378.4 4.5 multiply_reduce_fusion.4
  1403.4 5.1 fusion.299
  1426.1 4.5 multiply_reduce_fusion.4
  1451.1 5.1 fusion.299
  1473.9 4.5 multiply_reduce_fusion.4
  1498.9 5.0 fusion.299
  1521.7 4.5 multiply_reduce_fusion.4
  1546.7 5.1 fusion.299
  1571.6 4.2 fusion.107
  1587.5 4.6 fusion.128
  1592.1 4.6 fusion.129
  1596.7 4.6 fusion.127
  1601.3 4.5 fusion.123
  1605.8 4.7 fusion.125
  1610.5 16.8 add_convert_fusion
  1637.7 5.0 fusion.157
  1663.0 4.9 fusion.156
  1673.3 4.4 convolution_bitcast_fusion.10
  1679.6 39.5 %reduce-scatter.18.cloned.1.call-done = bf16[512,1024]{1,0:T(8,128)(2,1)} async-done(((bf16[2048,1024]{1,0:T(8,128)(2,1)}), bf16[512,1024]{1,0:T(8,128)(2,1)}) %reduce-scatter.18.cloned.1.call-update) | async-done | bytes 1048592 | tf_op jit(solution)/shard_map/reduce_scatter | solution.py:310
  1723.2 6.2 all-to-all-start.1
  1735.7 18.9 all-to-all-done.1
  1754.6 4.6 all-to-all-start.3
  1759.2 25.0 all-to-all-done.3
  1784.1 64.0 %reduce-scatter.36.cloned.1.call-done = f32[128,32]{0,1:T(8,128)} async-done(((f32[128,1024]{0,1:T(8,128)}), f32[128,32]{0,1:T(8,128)}) %reduce-scatter.36.cloned.1.call-update) | async-done | bytes 16400 | tf_op jit(solution)/shard_map/reduce_scatter | solution.py:564
  1848.2 133.5 %reduce-scatter.32.cloned.1.call-done = f32[2,32,128]{2,1,0:T(8,128)} async-done(((f32[2,1024,128]{2,1,0:T(8,128)}), f32[2,32,128]{2,1,0:T(8,128)}) %reduce-scatter.32.cloned.1.call-update) | async-done | bytes 32784 | tf_op jit(solution)/shard_map/reduce_scatter | solution.py:561
  1981.7 134.1 %reduce-scatter.38.cloned.1.call-done = f32[88,128]{1,0:T(8,128)} async-done(((f32[2816,128]{1,0:T(8,128)}), f32[88,128]{1,0:T(8,128)}) %reduce-scatter.38.cloned.1.call-update) | async-done | bytes 45072
  2115.7 136.6 %reduce-scatter.34.cloned.1.call-done = f32[2,128,88]{1,2,0:T(8,128)} async-done(((f32[2,128,2816]{1,2,0:T(8,128)}), f32[2,128,88]{1,2,0:T(8,128)}) %reduce-scatter.34.cloned.1.call-update) | async-done | bytes 90128 | tf_op jit(solution)/shard_map/reduce_scatter | solution.py:562
  2252.3 132.4 %reduce-scatter.28.cloned.1.call-done = f32[32,128]{1,0:T(8,128)} async-done(((f32[1024,128]{1,0:T(8,128)}), f32[32,128]{1,0:T(8,128)}) %reduce-scatter.28.cloned.1.call-update) | async-done | bytes 16400 | tf_op jit(solution)/shard_map/reduce_scatter | solution.py:559
  2384.8 132.2 %reduce-scatter.30.cloned.1.call-done = f32[128,32]{0,1:T(8,128)} async-done(((f32[128,1024]{0,1:T(8,128)}), f32[128,32]{0,1:T(8,128)}) %reduce-scatter.30.cloned.1.call-update) | async-done | bytes 16400 | tf_op jit(solution)/shard_map/reduce_scatter | solution.py:560
  2517.0 134.2 %reduce-scatter.26.cloned.1.call-done = f32[3,128,32]{1,2,0:T(8,128)} async-done(((f32[3,128,1024]{1,2,0:T(8,128)}), f32[3,128,32]{1,2,0:T(8,128)}) %reduce-scatter.26.cloned.1.call-update) | async-done | bytes 49168 | tf_op jit(solution)/shard_map/reduce_scatter | solution.py:558
  2651.2 134.0 %reduce-scatter.24.cloned.1.call-done = f32[3,32,128]{2,1,0:T(8,128)} async-done(((f32[3,1024,128]{2,1,0:T(8,128)}), f32[3,32,128]{2,1,0:T(8,128)}) %reduce-scatter.24.cloned.1.call-update) | async-done | bytes 49168 | tf_op jit(solution)/shard_map/reduce_scatter | solution.py:557
  (1143 shorter events, 938.3 us)
Async XLA Ops:
  7.2 39.1 %copy-start.74 = (f32[1024]{0:T(1024)S(1)}, f32[1024]{0:T(1024)}, u32[]{:S(2)}) copy-start(f32[1024]{0:T(1024)} %param.32) | copy-start | bytes 12292
  7.2 231.0 %all-gather.11.cloned.1.call-start = ((), (), s32[]{:S(2)}) async-start(), calls=%async_computation.17 | async-start | bytes 1769472 | tf_op jit(solution)/shard_map/all_gather | solution.py:402
  7.9 230.3 %all-gather.9.cloned.1.call-start = ((), (), s32[]{:S(2)}) async-start(), calls=%async_computation.16 | async-start | bytes 5242880 | tf_op jit(solution)/shard_map/all_gather | solution.py:187
  45.8 932.1 %copy-start.1 = (bf16[8,64,1024]{2,1,0:T(8,128)(2,1)}, bf16[8,64,1024]{2,1,0:T(8,128)(2,1)S(1)}, u32[]{:S(2)}) copy-start(bf16[8,64,1024]{2,1,0:T(8,128)(2,1)S(1)} %all_to_all.20) | copy-start | bytes 3145732
  45.9 44.1 %copy-start.90 = (bf16[128,32]{0,1:T(8,128)(2,1)S(1)}, bf16[128,32]{0,1:T(8,128)(2,1)}, u32[]{:S(2)}) copy-start(bf16[128,32]{0,1:T(8,128)(2,1)} %param.47) | copy-start | bytes 24580
  46.2 81.6 %copy-start.73 = (bf16[256,128]{1,0:T(8,128)(2,1)S(1)}, bf16[256,128]{1,0:T(8,128)(2,1)}, u32[]{:S(2)}) copy-start(bf16[256,128]{1,0:T(8,128)(2,1)} %param.35) | copy-start | bytes 196612
  46.3 111.3 %copy-start.78 = (bf16[3,32,128]{2,1,0:T(8,128)(2,1)S(1)}, bf16[3,32,128]{2,1,0:T(8,128)(2,1)}, u32[]{:S(2)}) copy-start(bf16[3,32,128]{2,1,0:T(8,128)(2,1)} %param.44) | copy-start | bytes 73732
  47.6 149.1 %copy-start.79 = (bf16[3,128,32]{1,2,0:T(8,128)(2,1)S(1)}, bf16[3,128,32]{1,2,0:T(8,128)(2,1)}, u32[]{:S(2)}) copy-start(bf16[3,128,32]{1,2,0:T(8,128)(2,1)} %param.45) | copy-start | bytes 73732
  47.6 600.2 %reduce-scatter.16.cloned.1.call-start = ((), (), s32[]{:S(2)}) async-start(), calls=%async_computation.18 | async-start | bytes 5242880 | tf_op jit(solution)/shard_map/reduce_scatter | solution.py:310
  48.3 79.5 %copy-start.62 = (s32[2048]{0:T(1024)}, s32[2048]{0:T(1024)S(1)}, u32[]{:S(2)}) copy-start(s32[2048]{0:T(1024)S(1)} %broadcast_add_fusion) | copy-start | bytes 24580
  48.4 193.5 %copy-start.92 = (s32[2048]{0:T(1024)}, s32[2048]{0:T(1024)S(1)}, u32[]{:S(2)}) copy-start(s32[2048]{0:T(1024)S(1)} %get-tuple-element.902) | copy-start | bytes 24580
  49.1 192.9 %copy-start.118 = (s32[128]{0:T(128)}, s32[128]{0:T(128)S(1)}, u32[]{:S(2)}) copy-start(s32[128]{0:T(128)S(1)} %and_select_fusion) | copy-start | bytes 1540
  196.7 45.3 %copy-start.44 = (bf16[3,1024,128]{2,1,0:T(8,128)(2,1)}, bf16[3,1024,128]{2,1,0:T(8,128)(2,1)S(1)}, u32[]{:S(2)}) copy-start(bf16[3,1024,128]{2,1,0:T(8,128)(2,1)S(1)} %all_gather.50) | copy-start | bytes 2359300
  253.3 5.7 copy-start.93
  253.3 5.7 copy-start.119
  275.0 5.8 copy-start.94
  275.0 5.8 copy-start.120
  602.0 176.5 %all-gather.19.cloned.1.call-start = ((), (), s32[]{:S(2)}) async-start(), calls=%async_computation.22 | async-start | bytes 1622016 | tf_op jit(solution)/shard_map/all_gather | solution.py:405
  602.6 176.0 %all-gather.21.cloned.1.call-start = ((), (), s32[]{:S(2)}) async-start(), calls=%async_computation.24 | async-start | bytes 5242880 | tf_op jit(solution)/shard_map/all_gather | solution.py:331
  636.4 13.1 copy-start.71
  636.5 154.1 %all-gather.13.cloned.1.call-start = ((), (), s32[]{:S(2)}) async-start(), calls=%async_computation.19 | async-start | bytes 5242880 | tf_op jit(solution)/shard_map/all_gather | solution.py:187
  649.6 328.4 %copy-start.76 = (f32[512]{0:T(512)}, f32[512]{0:T(512)S(1)}, u32[]{:S(2)}) copy-start(f32[512]{0:T(512)S(1)} %fusion.149) | copy-start | bytes 6148
  649.6 45.1 %copy-start.91 = (bf16[128,32]{0,1:T(8,128)(2,1)S(1)}, bf16[128,32]{0,1:T(8,128)(2,1)}, u32[]{:S(2)}) copy-start(bf16[128,32]{0,1:T(8,128)(2,1)} %param.51) | copy-start | bytes 24580
  649.6 85.8 %copy-start.80 = (bf16[88,128]{1,0:T(8,128)(2,1)S(1)}, bf16[88,128]{1,0:T(8,128)(2,1)}, u32[]{:S(2)}) copy-start(bf16[88,128]{1,0:T(8,128)(2,1)} %param.50) | copy-start | bytes 67588
  651.0 185.1 %all-gather.15.cloned.1.call-start = ((), (), s32[]{:S(2)}) async-start(), calls=%async_computation.20 | async-start | bytes 3244032 | tf_op jit(solution)/shard_map/all_gather | solution.py:404
  651.8 240.7 %all-gather.17.cloned.1.call-start = ((), (), s32[]{:S(2)}) async-start(), calls=%async_computation.21 | async-start | bytes 1486848 | tf_op jit(solution)/shard_map/all_gather | solution.py:413
  652.5 323.5 %reduce-scatter.20.cloned.1.call-start = ((), (), s32[]{:S(2)}) async-start(), calls=%async_computation.25 | async-start | bytes 5242880 | tf_op jit(solution)/shard_map/reduce_scatter | solution.py:191
  778.6 5.6 copy-start.33
  778.6 5.6 copy-start.59
  836.1 8.5 copy-start.11
  836.1 8.5 copy-start.99
  908.9 5.9 copy-start.110
  917.0 5.8 copy-start.48
  932.4 82.1 %all-gather.23.cloned.1.call-start = ((), (), s32[]{:S(2)}) async-start(), calls=%async_computation.26 | async-start | bytes 5242880 | tf_op jit(solution)/shard_map/all_gather | solution.py:331
  979.9 697.9 %reduce-scatter.22.cloned.1.call-start = ((), (), s32[]{:S(2)}) async-start(), calls=%async_computation.27 | async-start | bytes 5242880 | tf_op jit(solution)/shard_map/reduce_scatter | solution.py:191
  980.8 37.4 %copy-start.95 = (s32[2048]{0:T(1024)S(1)}, s32[2048]{0:T(1024)}, u32[]{:S(2)}) copy-start(s32[2048]{0:T(1024)} %copy-done.92) | copy-start | bytes 24580
  980.8 37.4 %copy-start.121 = (s32[128]{0:T(128)S(1)}, s32[128]{0:T(128)}, u32[]{:S(2)}) copy-start(s32[128]{0:T(128)} %copy-done.118) | copy-start | bytes 1540
  1353.4 12.0 copy-start.18
  1372.6 191.3 %copy-start.66 = (f32[2048,2]{0,1:T(2,128)S(1)}, f32[2048,2]{0,1:T(2,128)}, u32[]{:S(2)}) copy-start(f32[2048,2]{0,1:T(2,128)} %copy-done.65) | copy-start | bytes 49156
  1372.8 5.6 copy-start.13
  1563.9 7.6 copy-start.68
  1582.6 27.9 copy-start.26
  1584.2 7.8 copy-start.42
  1585.9 6.2 copy-start.40
  1587.5 9.2 copy-start.38
  1627.3 91.8 %reduce-scatter.18.cloned.1.call-start = ((), (), s32[]{:S(2)}) async-start(), calls=%async_computation.23 | async-start | bytes 5242880 | tf_op jit(solution)/shard_map/reduce_scatter | solution.py:310
  1637.7 210.5 %reduce-scatter.36.cloned.1.call-start = ((), (), s32[]{:S(2)}) async-start(), calls=%async_computation.34 | async-start | bytes 540672 | tf_op jit(solution)/shard_map/reduce_scatter | solution.py:564
  1642.7 338.9 %reduce-scatter.32.cloned.1.call-start = ((), (), s32[]{:S(2)}) async-start(), calls=%async_computation.32 | async-start | bytes 1081344 | tf_op jit(solution)/shard_map/reduce_scatter | solution.py:561
  1648.8 466.9 %reduce-scatter.38.cloned.1.call-start = ((), (), s32[]{:S(2)}) async-start(), calls=%async_computation.35 | async-start | bytes 1486848
  1653.0 599.4 %reduce-scatter.34.cloned.1.call-start = ((), (), s32[]{:S(2)}) async-start(), calls=%async_computation.33 | async-start | bytes 2973696 | tf_op jit(solution)/shard_map/reduce_scatter | solution.py:562
  1659.9 724.9 %reduce-scatter.28.cloned.1.call-start = ((), (), s32[]{:S(2)}) async-start(), calls=%async_computation.30 | async-start | bytes 540672 | tf_op jit(solution)/shard_map/reduce_scatter | solution.py:559
  1662.9 854.1 %reduce-scatter.30.cloned.1.call-start = ((), (), s32[]{:S(2)}) async-start(), calls=%async_computation.31 | async-start | bytes 540672 | tf_op jit(solution)/shard_map/reduce_scatter | solution.py:560
  1668.0 983.3 %reduce-scatter.26.cloned.1.call-start = ((), (), s32[]{:S(2)}) async-start(), calls=%async_computation.29 | async-start | bytes 1622016 | tf_op jit(solution)/shard_map/reduce_scatter | solution.py:558
  1673.3 6.3 copy-start.82
  1677.7 41.4 %copy-start.9 = (bf16[512,1024]{1,0:T(8,128)(2,1)S(1)}, bf16[512,1024]{1,0:T(8,128)(2,1)}, u32[]{:S(2)}) copy-start(bf16[512,1024]{1,0:T(8,128)(2,1)} %reduce-scatter.16.cloned.1.call-done) | copy-start | bytes 3145732
  1677.7 41.4 %copy-start.22 = (bf16[8,64,1024]{2,1,0:T(8,128)(2,1)S(1)}, bf16[8,64,1024]{2,1,0:T(8,128)(2,1)}, u32[]{:S(2)}) copy-start(bf16[8,64,1024]{2,1,0:T(8,128)(2,1)} %all_to_all.21) | copy-start | bytes 3145732
  1677.7 41.4 %copy-start.72 = (f32[1024]{0:T(1024)S(1)}, f32[1024]{0:T(1024)}, u32[]{:S(2)}) copy-start(f32[1024]{0:T(1024)} %param.33) | copy-start | bytes 12292
  1677.7 41.4 %copy-start.77 = (f32[512]{0:T(512)S(1)}, f32[512]{0:T(512)}, u32[]{:S(2)}) copy-start(f32[512]{0:T(512)} %copy-done.76) | copy-start | bytes 6148
  1677.7 41.4 %copy-start.84 = (f32[512]{0:T(512)S(1)}, f32[512]{0:T(512)}, u32[]{:S(2)}) copy-start(f32[512]{0:T(512)} %copy-done.83) | copy-start | bytes 6148
  1677.7 41.4 %copy-start.86 = (f32[512]{0:T(512)S(1)}, f32[512]{0:T(512)}, u32[]{:S(2)}) copy-start(f32[512]{0:T(512)} %copy-done.85) | copy-start | bytes 6148
  1723.2 6.2 copy-start.41
  1723.2 31.4 %all-to-all-start.1 = ((bf16[8,64,1024]{2,1,0:T(8,128)(2,1)}), bf16[8,64,1024]{2,1,0:T(8,128)(2,1)S(1)}, u32[]{:S(2)}, u32[]{:S(2)}) async-start(bf16[8,64,1024]{2,1,0:T(8,128)(2,1)} %bitcast.442), calls=%async_computation.3 | async-start | bytes 2097152 | tf_op jit(solution)/shard_map/all_to_all | solution.py:541
  1729.4 1055.8 %reduce-scatter.24.cloned.1.call-start = ((), (), s32[]{:S(2)}) async-start(), calls=%async_computation.28 | async-start | bytes 1622016 | tf_op jit(solution)/shard_map/reduce_scatter | solution.py:557
  1754.6 29.5 %all-to-all-start.3 = ((bf16[8,64,1024]{2,1,0:T(8,128)(2,1)}), bf16[8,64,1024]{2,1,0:T(8,128)(2,1)S(1)}, u32[]{:S(2)}, u32[]{:S(2)}) async-start(bf16[8,64,1024]{2,1,0:T(8,128)(2,1)} %bitcast.47), calls=%async_computation.7 | async-start | bytes 2097152 | tf_op jit(solution)/shard_map/all_to_all | solution.py:548
  (91 other events, 254.5 us)
Sparse Core Ops, SparseCore 0:
  10.2 51.9 all-gather.10
  64.4 35.1 all-gather.8
  602.2 45.6 reduce-scatter.15
  649.9 44.3 all-gather.18
  695.7 35.1 all-gather.20
  733.0 40.2 all-gather.12
  775.5 60.5 all-gather.14
  839.4 52.9 all-gather.16
  932.5 43.4 reduce-scatter.19
  980.0 34.4 all-gather.22
  1627.4 44.5 reduce-scatter.21
  1674.5 44.5 reduce-scatter.17
  1721.9 126.2 reduce-scatter.35
  1850.9 130.6 reduce-scatter.31
  1984.3 131.3 reduce-scatter.37
  2118.5 133.7 reduce-scatter.33
  2255.1 129.6 reduce-scatter.27
  2387.5 129.5 reduce-scatter.29
  2519.9 131.2 reduce-scatter.25
  2653.9 131.2 reduce-scatter.23
where the time goes:
time: 2820 us; the launch traced here: 2790 us
  waiting for transfers between devices  1260 us (45%)
  matrix products  694 us (25%)
  blocking collectives  385 us (14%)
  local copies, waits for them, and re-layouts  326 us (12%)
  other arithmetic  96.9 us (3%)
    dot_general x96, matrix products, advance(): jnp.einsum('thd,hde->the', query_stretch, memory_state, precision=highest)  154 us
    dot_general x128, matrix products, advance(): jnp.einsum('thd,hde->the', key_stretch, memory_state, precision=highest)  143 us
    unnamed x21, waiting for transfers between devices  137 us
    reduce_scatter x1, waiting for transfers between devices, per_device(): lax.psum_scatter(ffn_b_term, ('dp', 'tensor'), scatter_dimension=2, tiled...  137 us
    reduce_scatter x1, waiting for transfers between devices, per_device(): lax.psum_scatter(qkv_b_term, ('dp', 'tensor'), scatter_dimension=2, tiled...  134 us
    reduce_scatter x1, waiting for transfers between devices, per_device(): lax.psum_scatter(qkv_a_term, ('dp', 'tensor'), scatter_dimension=1, tiled...  134 us
    reduce_scatter x1, waiting for transfers between devices, per_device(): lax.psum_scatter(ffn_a_term, ('dp', 'tensor'), scatter_dimension=1, tiled...  133 us
    reduce_scatter x1, waiting for transfers between devices, per_device(): lax.psum_scatter(out_a_term, ('dp', 'tensor'), scatter_dimension=0, tiled...  132 us
  transfers between devices with their start and end apart: 22, of which 16 were waited for; matrix products, arithmetic and copies ran while one was open for 4% of the time, Pallas kernels for 0%

commit v1 on v0

--- a/solution.py
+++ b/solution.py
@@ -30,7 +30,8 @@
     members = lax.dynamic_slice_in_dim(sequence_permutation, group_number * SEQ_G, SEQ_G)
     member_length = pick_rows(sequence_length, members)
     member_adapter = pick_rows(sequence_adapter, members)
-    begins = jnp.cumsum(member_length) - member_length
+    order = jnp.arange(SEQ_G, dtype=jnp.int32)
+    begins = jnp.sum(jnp.where(order[None, :] < order[:, None], member_length[None, :], 0), 1)
     positions = jnp.arange(row_count, dtype=jnp.int32)
     seq_index = jnp.sum((positions[:, None] >= begins[None, :]).astype(jnp.int32), 1) - 1
     return (seq_index, pick_rows(member_adapter, seq_index), pick_rows(begins, seq_index))

time: 2820 us -> 2820 us (level)
  no operation moved by 1% of the time
where the time goes in v1:
time: 2820 us; the launch traced here: 2790 us
  waiting for transfers between devices  1260 us (45%)
  matrix products  694 us (25%)
  blocking collectives  385 us (14%)
  local copies, waits for them, and re-layouts  326 us (12%)
  other arithmetic  96.8 us (3%)
    dot_general x96, matrix products, advance(): jnp.einsum('thd,hde->the', query_stretch, memory_state, precision=highest)  154 us
    dot_general x128, matrix products, advance(): jnp.einsum('thd,hde->the', key_stretch, memory_state, precision=highest)  143 us
    unnamed x21, waiting for transfers between devices  137 us
    reduce_scatter x1, waiting for transfers between devices, per_device(): lax.psum_scatter(ffn_b_term, ('dp', 'tensor'), scatter_dimension=2, tiled...  137 us
    reduce_scatter x1, waiting for transfers between devices, per_device(): lax.psum_scatter(qkv_b_term, ('dp', 'tensor'), scatter_dimension=2, tiled...  134 us
    reduce_scatter x1, waiting for transfers between devices, per_device(): lax.psum_scatter(qkv_a_term, ('dp', 'tensor'), scatter_dimension=1, tiled...  134 us
    reduce_scatter x1, waiting for transfers between devices, per_device(): lax.psum_scatter(ffn_a_term, ('dp', 'tensor'), scatter_dimension=1, tiled...  133 us
    reduce_scatter x1, waiting for transfers between devices, per_device(): lax.psum_scatter(out_a_term, ('dp', 'tensor'), scatter_dimension=0, tiled...  132 us
  transfers between devices with their start and end apart: 22, of which 16 were waited for; matrix products, arithmetic and copies ran while one was open for 4% of the time, Pallas kernels for 0%

profile of v1, /device:TPU:2, one launch (start us, length us, event | category | flops | bytes accessed | tf_op | source)
XLA Modules:
  0.0 2794.2 jit_solution(5977338844136182775)
XLA Ops:
  8.0 37.9 %all_to_all.20 = bf16[8,64,1024]{2,1,0:T(8,128)(2,1)S(1)} all-to-all(bf16[8,64,1024]{2,1,0:T(8,128)(2,1)} %bitcast.441), channel_id=1, replica_groups=mesh['dp'=8,'tensor'=4] {'dp'}, dimensions={0} | all-to-all | bytes 2097152 | tf_op jit(solution)/shard_map/all_to_all | solution.py:385
  49.9 40.0 %all_gather.53 = bf16[1024,128]{1,0:T(8,128)(2,1)} all-gather(bf16[32,128]{1,0:T(8,128)(2,1)S(1)} %copy-done.89), channel_id=1, replica_groups=mesh['dp'=8,'tensor'=4] {'dp','tensor'}, dimensions={0}, use_global_device_ids=true | all-gather | bytes 270336 | tf_op jit(solution)/shard_map/all_gather | solution.py:411
  89.9 37.3 %all_gather.54 = bf16[128,1024]{0,1:T(8,128)(2,1)S(1)} all-gather(bf16[128,32]{0,1:T(8,128)(2,1)S(1)} %copy-done.90), channel_id=1, replica_groups=mesh['dp'=8,'tensor'=4] {'dp','tensor'}, dimensions={1}, use_global_device_ids=true | all-gather | bytes 270336 | tf_op jit(solution)/shard_map/all_gather | solution.py:412
  127.8 29.8 %all_gather.52 = bf16[256,1024]{1,0:T(8,128)(2,1)} all-gather(bf16[256,128]{1,0:T(8,128)(2,1)S(1)} %copy-done.73), channel_id=1, replica_groups=mesh['dp'=8,'tensor'=4] {'dp'}, dimensions={1}, use_global_device_ids=true | all-gather | bytes 589824 | tf_op jit(solution)/shard_map/all_gather | solution.py:404
  157.6 39.0 %all_gather.50 = bf16[3,1024,128]{2,1,0:T(8,128)(2,1)S(1)} all-gather(bf16[3,32,128]{2,1,0:T(8,128)(2,1)S(1)} %copy-done.78), channel_id=1, replica_groups=mesh['dp'=8,'tensor'=4] {'dp','tensor'}, dimensions={1}, use_global_device_ids=true | all-gather | bytes 811008 | tf_op jit(solution)/shard_map/all_gather | solution.py:409
  196.6 41.6 %all_gather.51 = bf16[3,128,1024]{1,2,0:T(8,128)(2,1)} all-gather(bf16[3,128,32]{1,2,0:T(8,128)(2,1)S(1)} %copy-done.79), channel_id=1, replica_groups=mesh['dp'=8,'tensor'=4] {'dp','tensor'}, dimensions={2}, use_global_device_ids=true | all-gather | bytes 811008 | tf_op jit(solution)/shard_map/all_gather | solution.py:410
  275.0 4.1 broadcast_multiply_fusion.1
  289.1 4.5 reshape.432
  293.6 5.0 copy.179
  300.3 233.1 %while.67 = (s32[]{:T(128)}, f32[2,128,128]{2,1,0:T(8,128)S(1)}, f32[32,64,2,128]{3,1,2,0:T(8,128)}, f32[32,2,128,128]{3,2,1,0:T(8,128)}, f32[2,1,1]{0,2,1:T(1,1...) while((s32[]{:T(128)}, f32[2,128,128]{2,1,0:T(8,128)S(1)}, ...), condition=%wide.region_14.15_spmd.clone, body=%wide.region_13.14_spmd.clone.sunk | while | flops 75841536 | bytes 1249960 | solution.py:64
  542.4 50.3 %while.65 = (s32[]{:T(128)}, f32[4,512,2,128]{3,2,1,0:T(2,128)}, f32[4,2,512,1]{2,1,3,0:T(2,128)}, s32[4]{0:T(128)S(1)}, bf16[3072,2,128]{2,0,1:T(8,128)(2,1)}, ...) while((s32[]{:T(128)}, f32[4,512,2,128]{3,2,1,0:T(2,128)}, ...), condition=%wide.region_9.10_spmd, body=%wide.region_6.9_spmd.sunk | while | flops 825753088 | bytes 32833268 | solution.py:125
  603.2 33.2 %all_to_all.21 = bf16[8,64,1024]{2,1,0:T(8,128)(2,1)} all-to-all(bf16[8,64,1024]{2,1,0:T(8,128)(2,1)S(1)} %bitcast.442), channel_id=1, replica_groups=mesh['dp'=8,'tensor'=4] {'dp'}, dimensions={0} | all-to-all | bytes 2097152 | tf_op jit(solution)/shard_map/all_to_all | solution.py:392
  636.5 11.3 reduce-scatter.16.cloned.1.call-done
  652.5 42.2 %all_gather.57 = bf16[2,1024,128]{2,1,0:T(8,128)(2,1)} all-gather(bf16[2,32,128]{2,1,0:T(8,128)(2,1)S(1)} %copy-done.87), channel_id=1, replica_groups=mesh['dp'=8,'tensor'=4] {'dp','tensor'}, dimensions={1}, use_global_device_ids=true | all-gather | bytes 540672 | tf_op jit(solution)/shard_map/all_gather | solution.py:413
  694.7 40.7 %all_gather.61 = bf16[128,1024]{0,1:T(8,128)(2,1)} all-gather(bf16[128,32]{0,1:T(8,128)(2,1)S(1)} %copy-done.91), channel_id=1, replica_groups=mesh['dp'=8,'tensor'=4] {'dp','tensor'}, dimensions={1}, use_global_device_ids=true | all-gather | bytes 270336 | tf_op jit(solution)/shard_map/all_gather | solution.py:416
  735.4 43.1 %all_gather.60 = bf16[2816,128]{1,0:T(8,128)(2,1)} all-gather(bf16[88,128]{1,0:T(8,128)(2,1)S(1)} %copy-done.80), channel_id=1, replica_groups=mesh['dp'=8,'tensor'=4] {'dp','tensor'}, dimensions={0}, use_global_device_ids=true | all-gather | bytes 743424 | tf_op jit(solution)/shard_map/all_gather | solution.py:415
  778.5 5.6 fusion.154
  786.2 4.3 convolution_add_fusion.2
  790.5 4.4 fusion.91
  797.1 39.0 %all-gather.15.cloned.1.call-done = bf16[2,1024,704]{1,2,0:T(8,128)(2,1)} async-done(((bf16[2,128,704]{1,2,0:T(8,128)(2,1)}), bf16[2,1024,704]{1,2,0:T(8,128)(2,1)}) %all-gather.15.cloned.1.call-update) | async-done | bytes 2883600 | tf_op jit(solution)/shard_map/all_gather | solution.py:405
  836.1 8.5 fusion.121
  844.6 5.0 fusion.119
  849.6 42.8 %all-gather.17.cloned.1.call-done = bf16[2,128,2816]{1,2,0:T(8,128)(2,1)} async-done(((bf16[2,128,88]{1,2,0:T(8,128)(2,1)}), bf16[2,128,2816]{1,2,0:T(8,128)(2,1)}) %all-gather.17.cloned.1.call-update) | async-done | bytes 1441808 | tf_op jit(solution)/shard_map/all_gather | solution.py:414
  897.1 7.4 fusion.81
  908.9 5.9 fusion.118
  916.9 5.8 fusion.120
  922.7 9.6 add_convert_fusion.1
  932.4 43.6 %reduce-scatter.20.cloned.1.call-done = bf16[512,1024]{1,0:T(8,128)(2,1)} async-done(((bf16[2048,1024]{1,0:T(8,128)(2,1)}), bf16[512,1024]{1,0:T(8,128)(2,1)}) %reduce-scatter.20.cloned.1.call-update) | async-done | bytes 1048592 | tf_op jit(solution)/shard_map/reduce_scatter | solution.py:192
  980.8 33.7 %all-gather.23.cloned.1.call-done = bf16[2048,1024]{1,0:T(8,128)(2,1)} async-done(((bf16[512,1024]{1,0:T(8,128)(2,1)}), bf16[2048,1024]{1,0:T(8,128)(2,1)}) %all-gather.23.cloned.1.call-update) | async-done | bytes 4194320 | tf_op jit(solution)/shard_map/all_gather | solution.py:332
  1024.9 4.6 copy.188
  1034.3 315.6 %while.68 = (s32[]{:T(128)}, f32[2,128,128]{2,1,0:T(8,128)S(1)}, f32[32,64,2,128]{3,1,2,0:T(8,128)}, f32[32,64,2,128]{3,1,2,0:T(8,128)}, f32[32,64,2,128]{3,1,0,...) while((s32[]{:T(128)}, f32[2,128,128]{2,1,0:T(8,128)S(1)}, ...), condition=%wide.region_24.25_spmd.clone, body=%wide.region_23.24_spmd.clone.sunk | while | flops 176668672 | bytes 3343587 | solution.py:64
  1353.3 12.0 fusion.116
  1372.5 191.3 %while.66 = (s32[]{:T(128)}, f32[2048,2,128]{2,0,1:T(8,128)}, f32[3072,2,128]{2,0,1:T(8,128)}, f32[3072,2,128]{2,0,1:T(8,128)}, bf16[3072,2,128]{2,0,1:T(8,128)(...) while((s32[]{:T(128)}, f32[2048,2,128]{2,0,1:T(8,128)}, ...), condition=%wide.region_22.23_spmd, body=%wide.region_20.22_spmd.sunk | while | flops 2036596224 | bytes 127716200 | solution.py:183
  1378.3 4.5 multiply_reduce_fusion.4
  1403.3 5.1 fusion.299
  1426.1 4.5 multiply_reduce_fusion.4
  1451.1 5.1 fusion.299
  1473.9 4.5 multiply_reduce_fusion.4
  1498.8 5.0 fusion.299
  1521.6 4.5 multiply_reduce_fusion.4
  1546.6 5.1 fusion.299
  1571.5 4.2 fusion.107
  1587.5 4.6 fusion.128
  1592.0 4.6 fusion.129
  1596.6 4.6 fusion.127
  1601.2 4.5 fusion.123
  1605.8 4.7 fusion.125
  1610.5 16.8 add_convert_fusion
  1637.7 5.0 fusion.157
  1662.9 4.9 fusion.156
  1673.2 4.4 convolution_bitcast_fusion.10
  1679.5 39.5 %reduce-scatter.18.cloned.1.call-done = bf16[512,1024]{1,0:T(8,128)(2,1)} async-done(((bf16[2048,1024]{1,0:T(8,128)(2,1)}), bf16[512,1024]{1,0:T(8,128)(2,1)}) %reduce-scatter.18.cloned.1.call-update) | async-done | bytes 1048592 | tf_op jit(solution)/shard_map/reduce_scatter | solution.py:311
  1723.2 6.2 all-to-all-start.1
  1735.6 18.9 all-to-all-done.1
  1754.6 4.6 all-to-all-start.3
  1759.1 25.0 all-to-all-done.3
  1784.1 64.0 %reduce-scatter.36.cloned.1.call-done = f32[128,32]{0,1:T(8,128)} async-done(((f32[128,1024]{0,1:T(8,128)}), f32[128,32]{0,1:T(8,128)}) %reduce-scatter.36.cloned.1.call-update) | async-done | bytes 16400 | tf_op jit(solution)/shard_map/reduce_scatter | solution.py:565
  1848.1 133.5 %reduce-scatter.32.cloned.1.call-done = f32[2,32,128]{2,1,0:T(8,128)} async-done(((f32[2,1024,128]{2,1,0:T(8,128)}), f32[2,32,128]{2,1,0:T(8,128)}) %reduce-scatter.32.cloned.1.call-update) | async-done | bytes 32784 | tf_op jit(solution)/shard_map/reduce_scatter | solution.py:562
  1981.6 134.1 %reduce-scatter.38.cloned.1.call-done = f32[88,128]{1,0:T(8,128)} async-done(((f32[2816,128]{1,0:T(8,128)}), f32[88,128]{1,0:T(8,128)}) %reduce-scatter.38.cloned.1.call-update) | async-done | bytes 45072
  2115.7 136.6 %reduce-scatter.34.cloned.1.call-done = f32[2,128,88]{1,2,0:T(8,128)} async-done(((f32[2,128,2816]{1,2,0:T(8,128)}), f32[2,128,88]{1,2,0:T(8,128)}) %reduce-scatter.34.cloned.1.call-update) | async-done | bytes 90128 | tf_op jit(solution)/shard_map/reduce_scatter | solution.py:563
  2252.3 132.4 %reduce-scatter.28.cloned.1.call-done = f32[32,128]{1,0:T(8,128)} async-done(((f32[1024,128]{1,0:T(8,128)}), f32[32,128]{1,0:T(8,128)}) %reduce-scatter.28.cloned.1.call-update) | async-done | bytes 16400 | tf_op jit(solution)/shard_map/reduce_scatter | solution.py:560
  2384.7 132.2 %reduce-scatter.30.cloned.1.call-done = f32[128,32]{0,1:T(8,128)} async-done(((f32[128,1024]{0,1:T(8,128)}), f32[128,32]{0,1:T(8,128)}) %reduce-scatter.30.cloned.1.call-update) | async-done | bytes 16400 | tf_op jit(solution)/shard_map/reduce_scatter | solution.py:561
  2517.0 134.2 %reduce-scatter.26.cloned.1.call-done = f32[3,128,32]{1,2,0:T(8,128)} async-done(((f32[3,128,1024]{1,2,0:T(8,128)}), f32[3,128,32]{1,2,0:T(8,128)}) %reduce-scatter.26.cloned.1.call-update) | async-done | bytes 49168 | tf_op jit(solution)/shard_map/reduce_scatter | solution.py:559
  2651.2 134.0 %reduce-scatter.24.cloned.1.call-done = f32[3,32,128]{2,1,0:T(8,128)} async-done(((f32[3,1024,128]{2,1,0:T(8,128)}), f32[3,32,128]{2,1,0:T(8,128)}) %reduce-scatter.24.cloned.1.call-update) | async-done | bytes 49168 | tf_op jit(solution)/shard_map/reduce_scatter | solution.py:558
  (1142 shorter events, 938.2 us)
Async XLA Ops:
  7.2 39.1 %copy-start.74 = (f32[1024]{0:T(1024)S(1)}, f32[1024]{0:T(1024)}, u32[]{:S(2)}) copy-start(f32[1024]{0:T(1024)} %param.32) | copy-start | bytes 12292
  7.2 231.0 %all-gather.11.cloned.1.call-start = ((), (), s32[]{:S(2)}) async-start(), calls=%async_computation.17 | async-start | bytes 1769472 | tf_op jit(solution)/shard_map/all_gather | solution.py:403
  7.9 230.2 %all-gather.9.cloned.1.call-start = ((), (), s32[]{:S(2)}) async-start(), calls=%async_computation.16 | async-start | bytes 5242880 | tf_op jit(solution)/shard_map/all_gather | solution.py:188
  45.8 932.1 %copy-start.1 = (bf16[8,64,1024]{2,1,0:T(8,128)(2,1)}, bf16[8,64,1024]{2,1,0:T(8,128)(2,1)S(1)}, u32[]{:S(2)}) copy-start(bf16[8,64,1024]{2,1,0:T(8,128)(2,1)S(1)} %all_to_all.20) | copy-start | bytes 3145732
  45.9 44.0 %copy-start.90 = (bf16[128,32]{0,1:T(8,128)(2,1)S(1)}, bf16[128,32]{0,1:T(8,128)(2,1)}, u32[]{:S(2)}) copy-start(bf16[128,32]{0,1:T(8,128)(2,1)} %param.47) | copy-start | bytes 24580
  46.2 81.6 %copy-start.73 = (bf16[256,128]{1,0:T(8,128)(2,1)S(1)}, bf16[256,128]{1,0:T(8,128)(2,1)}, u32[]{:S(2)}) copy-start(bf16[256,128]{1,0:T(8,128)(2,1)} %param.35) | copy-start | bytes 196612
  46.3 111.3 %copy-start.78 = (bf16[3,32,128]{2,1,0:T(8,128)(2,1)S(1)}, bf16[3,32,128]{2,1,0:T(8,128)(2,1)}, u32[]{:S(2)}) copy-start(bf16[3,32,128]{2,1,0:T(8,128)(2,1)} %param.44) | copy-start | bytes 73732
  47.6 149.0 %copy-start.79 = (bf16[3,128,32]{1,2,0:T(8,128)(2,1)S(1)}, bf16[3,128,32]{1,2,0:T(8,128)(2,1)}, u32[]{:S(2)}) copy-start(bf16[3,128,32]{1,2,0:T(8,128)(2,1)} %param.45) | copy-start | bytes 73732
  47.6 600.2 %reduce-scatter.16.cloned.1.call-start = ((), (), s32[]{:S(2)}) async-start(), calls=%async_computation.18 | async-start | bytes 5242880 | tf_op jit(solution)/shard_map/reduce_scatter | solution.py:311
  48.2 79.5 %copy-start.62 = (s32[2048]{0:T(1024)}, s32[2048]{0:T(1024)S(1)}, u32[]{:S(2)}) copy-start(s32[2048]{0:T(1024)S(1)} %broadcast_add_fusion) | copy-start | bytes 24580
  48.4 193.6 %copy-start.92 = (s32[2048]{0:T(1024)}, s32[2048]{0:T(1024)S(1)}, u32[]{:S(2)}) copy-start(s32[2048]{0:T(1024)S(1)} %get-tuple-element.902) | copy-start | bytes 24580
  49.0 192.9 %copy-start.118 = (s32[128]{0:T(128)}, s32[128]{0:T(128)S(1)}, u32[]{:S(2)}) copy-start(s32[128]{0:T(128)S(1)} %and_select_fusion) | copy-start | bytes 1540
  196.6 45.3 %copy-start.44 = (bf16[3,1024,128]{2,1,0:T(8,128)(2,1)}, bf16[3,1024,128]{2,1,0:T(8,128)(2,1)S(1)}, u32[]{:S(2)}) copy-start(bf16[3,1024,128]{2,1,0:T(8,128)(2,1)S(1)} %all_gather.50) | copy-start | bytes 2359300
  253.3 5.7 copy-start.93
  253.3 5.7 copy-start.119
  275.0 5.8 copy-start.94
  275.0 5.8 copy-start.120
  602.0 176.5 %all-gather.19.cloned.1.call-start = ((), (), s32[]{:S(2)}) async-start(), calls=%async_computation.22 | async-start | bytes 1622016 | tf_op jit(solution)/shard_map/all_gather | solution.py:406
  602.6 176.0 %all-gather.21.cloned.1.call-start = ((), (), s32[]{:S(2)}) async-start(), calls=%async_computation.24 | async-start | bytes 5242880 | tf_op jit(solution)/shard_map/all_gather | solution.py:332
  636.4 13.1 copy-start.71
  636.4 154.1 %all-gather.13.cloned.1.call-start = ((), (), s32[]{:S(2)}) async-start(), calls=%async_computation.19 | async-start | bytes 5242880 | tf_op jit(solution)/shard_map/all_gather | solution.py:188
  649.5 328.4 %copy-start.76 = (f32[512]{0:T(512)}, f32[512]{0:T(512)S(1)}, u32[]{:S(2)}) copy-start(f32[512]{0:T(512)S(1)} %fusion.149) | copy-start | bytes 6148
  649.6 45.1 %copy-start.91 = (bf16[128,32]{0,1:T(8,128)(2,1)S(1)}, bf16[128,32]{0,1:T(8,128)(2,1)}, u32[]{:S(2)}) copy-start(bf16[128,32]{0,1:T(8,128)(2,1)} %param.51) | copy-start | bytes 24580
  649.6 85.8 %copy-start.80 = (bf16[88,128]{1,0:T(8,128)(2,1)S(1)}, bf16[88,128]{1,0:T(8,128)(2,1)}, u32[]{:S(2)}) copy-start(bf16[88,128]{1,0:T(8,128)(2,1)} %param.50) | copy-start | bytes 67588
  651.0 185.1 %all-gather.15.cloned.1.call-start = ((), (), s32[]{:S(2)}) async-start(), calls=%async_computation.20 | async-start | bytes 3244032 | tf_op jit(solution)/shard_map/all_gather | solution.py:405
  651.7 240.7 %all-gather.17.cloned.1.call-start = ((), (), s32[]{:S(2)}) async-start(), calls=%async_computation.21 | async-start | bytes 1486848 | tf_op jit(solution)/shard_map/all_gather | solution.py:414
  652.5 323.5 %reduce-scatter.20.cloned.1.call-start = ((), (), s32[]{:S(2)}) async-start(), calls=%async_computation.25 | async-start | bytes 5242880 | tf_op jit(solution)/shard_map/reduce_scatter | solution.py:192
  778.5 5.6 copy-start.33
  778.5 5.6 copy-start.59
  836.1 8.5 copy-start.11
  836.1 8.5 copy-start.99
  908.9 5.9 copy-start.110
  916.9 5.8 copy-start.48
  932.3 82.1 %all-gather.23.cloned.1.call-start = ((), (), s32[]{:S(2)}) async-start(), calls=%async_computation.26 | async-start | bytes 5242880 | tf_op jit(solution)/shard_map/all_gather | solution.py:332
  979.8 697.9 %reduce-scatter.22.cloned.1.call-start = ((), (), s32[]{:S(2)}) async-start(), calls=%async_computation.27 | async-start | bytes 5242880 | tf_op jit(solution)/shard_map/reduce_scatter | solution.py:192
  980.8 37.4 %copy-start.95 = (s32[2048]{0:T(1024)S(1)}, s32[2048]{0:T(1024)}, u32[]{:S(2)}) copy-start(s32[2048]{0:T(1024)} %copy-done.92) | copy-start | bytes 24580
  980.8 37.4 %copy-start.121 = (s32[128]{0:T(128)S(1)}, s32[128]{0:T(128)}, u32[]{:S(2)}) copy-start(s32[128]{0:T(128)} %copy-done.118) | copy-start | bytes 1540
  1353.3 12.0 copy-start.18
  1372.5 191.3 %copy-start.66 = (f32[2048,2]{0,1:T(2,128)S(1)}, f32[2048,2]{0,1:T(2,128)}, u32[]{:S(2)}) copy-start(f32[2048,2]{0,1:T(2,128)} %copy-done.65) | copy-start | bytes 49156
  1372.7 5.6 copy-start.13
  1563.9 7.6 copy-start.68
  1582.6 27.9 copy-start.26
  1584.2 7.8 copy-start.42
  1585.9 6.2 copy-start.40
  1587.4 9.2 copy-start.38
  1627.2 91.8 %reduce-scatter.18.cloned.1.call-start = ((), (), s32[]{:S(2)}) async-start(), calls=%async_computation.23 | async-start | bytes 5242880 | tf_op jit(solution)/shard_map/reduce_scatter | solution.py:311
  1637.6 210.5 %reduce-scatter.36.cloned.1.call-start = ((), (), s32[]{:S(2)}) async-start(), calls=%async_computation.34 | async-start | bytes 540672 | tf_op jit(solution)/shard_map/reduce_scatter | solution.py:565
  1642.7 338.9 %reduce-scatter.32.cloned.1.call-start = ((), (), s32[]{:S(2)}) async-start(), calls=%async_computation.32 | async-start | bytes 1081344 | tf_op jit(solution)/shard_map/reduce_scatter | solution.py:562
  1648.8 466.9 %reduce-scatter.38.cloned.1.call-start = ((), (), s32[]{:S(2)}) async-start(), calls=%async_computation.35 | async-start | bytes 1486848
  1652.9 599.4 %reduce-scatter.34.cloned.1.call-start = ((), (), s32[]{:S(2)}) async-start(), calls=%async_computation.33 | async-start | bytes 2973696 | tf_op jit(solution)/shard_map/reduce_scatter | solution.py:563
  1659.8 724.9 %reduce-scatter.28.cloned.1.call-start = ((), (), s32[]{:S(2)}) async-start(), calls=%async_computation.30 | async-start | bytes 540672 | tf_op jit(solution)/shard_map/reduce_scatter | solution.py:560
  1662.9 854.1 %reduce-scatter.30.cloned.1.call-start = ((), (), s32[]{:S(2)}) async-start(), calls=%async_computation.31 | async-start | bytes 540672 | tf_op jit(solution)/shard_map/reduce_scatter | solution.py:561
  1667.9 983.3 %reduce-scatter.26.cloned.1.call-start = ((), (), s32[]{:S(2)}) async-start(), calls=%async_computation.29 | async-start | bytes 1622016 | tf_op jit(solution)/shard_map/reduce_scatter | solution.py:559
  1673.2 6.3 copy-start.82
  1677.7 41.4 %copy-start.9 = (bf16[512,1024]{1,0:T(8,128)(2,1)S(1)}, bf16[512,1024]{1,0:T(8,128)(2,1)}, u32[]{:S(2)}) copy-start(bf16[512,1024]{1,0:T(8,128)(2,1)} %reduce-scatter.16.cloned.1.call-done) | copy-start | bytes 3145732
  1677.7 41.4 %copy-start.22 = (bf16[8,64,1024]{2,1,0:T(8,128)(2,1)S(1)}, bf16[8,64,1024]{2,1,0:T(8,128)(2,1)}, u32[]{:S(2)}) copy-start(bf16[8,64,1024]{2,1,0:T(8,128)(2,1)} %all_to_all.21) | copy-start | bytes 3145732
  1677.7 41.4 %copy-start.72 = (f32[1024]{0:T(1024)S(1)}, f32[1024]{0:T(1024)}, u32[]{:S(2)}) copy-start(f32[1024]{0:T(1024)} %param.33) | copy-start | bytes 12292
  1677.7 41.4 %copy-start.77 = (f32[512]{0:T(512)S(1)}, f32[512]{0:T(512)}, u32[]{:S(2)}) copy-start(f32[512]{0:T(512)} %copy-done.76) | copy-start | bytes 6148
  1677.7 41.4 %copy-start.84 = (f32[512]{0:T(512)S(1)}, f32[512]{0:T(512)}, u32[]{:S(2)}) copy-start(f32[512]{0:T(512)} %copy-done.83) | copy-start | bytes 6148
  1677.7 41.4 %copy-start.86 = (f32[512]{0:T(512)S(1)}, f32[512]{0:T(512)}, u32[]{:S(2)}) copy-start(f32[512]{0:T(512)} %copy-done.85) | copy-start | bytes 6148
  1723.2 6.2 copy-start.41
  1723.2 31.4 %all-to-all-start.1 = ((bf16[8,64,1024]{2,1,0:T(8,128)(2,1)}), bf16[8,64,1024]{2,1,0:T(8,128)(2,1)S(1)}, u32[]{:S(2)}, u32[]{:S(2)}) async-start(bf16[8,64,1024]{2,1,0:T(8,128)(2,1)} %bitcast.439), calls=%async_computation.3 | async-start | bytes 2097152 | tf_op jit(solution)/shard_map/all_to_all | solution.py:542
  1729.4 1055.8 %reduce-scatter.24.cloned.1.call-start = ((), (), s32[]{:S(2)}) async-start(), calls=%async_computation.28 | async-start | bytes 1622016 | tf_op jit(solution)/shard_map/reduce_scatter | solution.py:558
  1754.6 29.5 %all-to-all-start.3 = ((bf16[8,64,1024]{2,1,0:T(8,128)(2,1)}), bf16[8,64,1024]{2,1,0:T(8,128)(2,1)S(1)}, u32[]{:S(2)}, u32[]{:S(2)}) async-start(bf16[8,64,1024]{2,1,0:T(8,128)(2,1)} %bitcast.45), calls=%async_computation.7 | async-start | bytes 2097152 | tf_op jit(solution)/shard_map/all_to_all | solution.py:549
  (91 other events, 254.2 us)
Sparse Core Ops, SparseCore 0:
  10.2 51.9 all-gather.10
  64.4 35.1 all-gather.8
  602.1 45.6 reduce-scatter.15
  649.9 44.2 all-gather.18
  695.7 35.1 all-gather.20
  732.9 40.2 all-gather.12
  775.5 60.5 all-gather.14
  839.4 52.9 all-gather.16
  932.4 43.4 reduce-scatter.19
  980.0 34.4 all-gather.22
  1627.4 44.5 reduce-scatter.21
  1674.5 44.5 reduce-scatter.17
  1721.8 126.2 reduce-scatter.35
  1850.9 130.6 reduce-scatter.31
  1984.3 131.3 reduce-scatter.37
  2118.5 133.7 reduce-scatter.33
  2255.0 129.6 reduce-scatter.27
  2387.4 129.5 reduce-scatter.29
  2519.9 131.2 reduce-scatter.25
  2653.9 131.2 reduce-scatter.23

commit v2 on v0

v2 whole, which is shorter than its diff:
```python
import functools

import jax
import jax.numpy as jnp
from jax import lax
from jax.experimental import pallas as pl
from jax.experimental.pallas import tpu as pltpu
from jax.sharding import PartitionSpec as P

HEAD_DIM = 128
ADAPTER_RANK = 16
STRETCH = 64
SEQ_G = 3
LANES = 128
BLOCK = 256
MEMORY_GAIN = 32.0
EPSILON = 1e-06
LOG2E = 1.4426950408889634
BF16 = jnp.bfloat16
F32 = jnp.float32
VMEM_LIMIT = 56 * 1024 * 1024


def nn(left, right):
    return jnp.dot(left, right, preferred_element_type=F32)


def nt(left, right, precision=None):
    return lax.dot_general(
        left, right, (((1,), (1,)), ((), ())), precision=precision, preferred_element_type=F32
    )


def tn(left, right):
    return lax.dot_general(left, right, (((0,), (0,)), ((), ())), preferred_element_type=F32)


def params(vmem=VMEM_LIMIT):
    return pltpu.CompilerParams(dimension_semantics=("arbitrary",), vmem_limit_bytes=vmem)


def cost(flops, moved):
    return pl.CostEstimate(flops=int(flops), bytes_accessed=int(moved), transcendentals=0)


def whole(*shape):
    return pl.BlockSpec(shape, lambda *_: (0,) * len(shape), pipeline_mode=pl.Buffered(1))


def adapter_select(meta, first_row, rows, copies):
    row = first_row + lax.broadcasted_iota(jnp.int32, (rows, 1), 0)
    adapter = jnp.where(row >= meta[1], meta[4], jnp.where(row >= meta[0], meta[3], meta[2]))
    column = lax.broadcasted_iota(jnp.int32, (rows, copies * LANES), 1)
    return (column % LANES) // ADAPTER_RANK == adapter


def keep_low(select, values):
    return jnp.where(select, values, 0.0).astype(BF16)


def qkv_kernel(meta, x0, x1, x2, x3, gain, weight, lower, upper_t, normed, qkv, latent, x_scr):
    step = pl.program_id(0)
    rows = x_scr.shape[0]
    for k, x_ref in enumerate((x0, x1, x2, x3)):

        @pl.when(step == k)
        def _():
            x_scr[...] = x_ref[...]

    values = x_scr[...].astype(F32)
    scale = lax.rsqrt(jnp.mean(values * values, -1, keepdims=True) + EPSILON)
    low = (values * scale * gain[...]).astype(BF16)
    normed[...] = low
    select = adapter_select(meta, (meta[7] ^ step) * rows, rows, 3)
    lat = keep_low(select, nn(low, lower[...]))
    latent[...] = lat
    for m in range(3):
        qkv[m] = (
            nn(low, weight[m]) + nt(lat[:, m * LANES : (m + 1) * LANES], upper_t[m])
        ).astype(BF16)


def project_qkv(meta, pieces, gain, weight, lower, upper_t):
    rows, width = pieces[0].shape
    own = weight.shape[2]
    total = rows * len(pieces)
    place = lambda step, meta: (meta[7] ^ step, 0)
    return pl.pallas_call(
        qkv_kernel,
        grid_spec=pltpu.PrefetchScalarGridSpec(
            num_scalar_prefetch=1,
            grid=(len(pieces),),
            in_specs=[whole(rows, width)] * 4
            + [
                whole(1, width),
                whole(*weight.shape),
                whole(*lower.shape),
                whole(*upper_t.shape),
            ],
            out_specs=[
                pl.BlockSpec((rows, width), place),
                pl.BlockSpec((3, rows, own), lambda step, meta: (0, meta[7] ^ step, 0)),
                pl.BlockSpec((rows, 3 * LANES), place),
            ],
            scratch_shapes=[pltpu.VMEM((rows, width), BF16)],
        ),
        out_shape=[
            jax.ShapeDtypeStruct((total, width), BF16),
            jax.ShapeDtypeStruct((3, total, own), BF16),
            jax.ShapeDtypeStruct((total, 3 * LANES), BF16),
        ],
        compiler_params=params(),
        cost_estimate=cost(2 * total * width * (3 * own + 600), 4 * total * width),
        name="project_qkv",
    )(meta, *pieces, gain, weight, lower, upper_t)


def span_variants(count, spans, run):
    for n, blocks in enumerate(spans):
        if n == 0:
            condition = count <= blocks
        else:
            condition = count == blocks
        pl.when(condition)(functools.partial(run, blocks * BLOCK))


def stretch_columns(low, total_stretches):
    stretch = lax.broadcasted_iota(jnp.int32, low.shape, 0) // STRETCH
    zero = jnp.zeros_like(low)
    return jnp.concatenate(
        [jnp.where(stretch == n, low, zero) for n in range(total_stretches)], 1
    )


def unit_rows(values):
    inverse = lax.rsqrt(jnp.sum(values * values, -1, keepdims=True) + EPSILON)
    return values * inverse, inverse


def mixer_forward_kernel(
    spans, meta, fmeta, qkv, heads, attended, log_total, states, state_scr
):
    block = pl.program_id(0)
    first_row = block * BLOCK
    start_two, start_three = meta[0], meta[1]
    row = first_row + lax.broadcasted_iota(jnp.int32, (BLOCK, 1), 0)
    begin = jnp.where(row >= start_three, start_three, jnp.where(row >= start_two, start_two, 0))
    first_begin = jnp.where(
        first_row >= start_three, start_three, jnp.where(first_row >= start_two, start_two, 0)
    )
    factor = HEAD_DIM ** (-0.5) * LOG2E
    stretches = BLOCK // STRETCH

    @pl.when(block == 0)
    def _():
        state_scr[...] = jnp.zeros_like(state_scr)

    for h in range(2):
        cols = slice(h * HEAD_DIM, (h + 1) * HEAD_DIM)
        window = meta[5 + h]
        low_key = jnp.maximum(row - window + 1, begin)
        first_key = jnp.maximum(first_row - window + 1, first_begin)
        count = block - first_key // BLOCK + 1

        def attend(span, cols=cols, low_key=low_key, h=h):
            start = pl.multiple_of(jnp.maximum(first_row + BLOCK - span, 0), BLOCK)
            query = qkv[0, pl.ds(pl.multiple_of(first_row, BLOCK), BLOCK), cols]
            key = qkv[1, pl.ds(start, span), cols]
            value = qkv[2, pl.ds(start, span), cols]
            score = nt(query, key)
            position = start + lax.broadcasted_iota(jnp.int32, (BLOCK, span), 1)
            score = jnp.where((position >= low_key) & (position <= row), score, -1e30)
            top = jnp.max(score, -1, keepdims=True)
            weight = jnp.exp2((score - top) * factor).astype(BF16)
            with_ones = jnp.concatenate([value, jnp.ones_like(value)], 1)
            both = nn(weight, with_ones)
            total = both[:, HEAD_DIM : HEAD_DIM + 1]
            attended[:, cols] = both[:, :HEAD_DIM] / both[:, HEAD_DIM:]
            logs = jnp.broadcast_to(top * factor + jnp.log2(total), (BLOCK, LANES))
            pick = jnp.where(lax.broadcasted_iota(jnp.int32, (8, LANES), 1) == 0, 1.0, 0.0)
            log_total[0, h : h + 1, :] = nt(pick, logs, lax.Precision.HIGHEST)[0:1]

        span_variants(count, spans, attend)

    for h in range(2):
        cols = slice(h * HEAD_DIM, (h + 1) * HEAD_DIM)
        here = pl.ds(pl.multiple_of(first_row, BLOCK), BLOCK)
        query_unit, _ = unit_rows(qkv[0, here, cols].astype(F32))
        key_unit, _ = unit_rows(qkv[1, here, cols].astype(F32))
        query_low = query_unit.astype(BF16)
        key_low = key_unit.astype(BF16)
        by_stretch = stretch_columns(key_low, stretches)
        retention, step_size = fmeta[h], fmeta[2 + h]
        gram = (nn(key_unit.T.astype(BF16), by_stretch) * step_size).astype(BF16)
        written = nn(qkv[2, here, cols].astype(F32).T.astype(BF16), by_stretch) * step_size
        state = state_scr[h]
        for n in range(stretches):
            row_at = first_row + n * STRETCH
            keep = jnp.where((row_at == start_two) | (row_at == start_three), 0.0, 1.0)
            state = state * keep
            low = state.astype(BF16)
            states[n, h] = low
            rows = slice(n * STRETCH, (n + 1) * STRETCH)
            lanes = slice(n * HEAD_DIM, (n + 1) * HEAD_DIM)
            read = nt(query_low[rows], low)
            heads[rows, cols] = (attended[rows, cols] + MEMORY_GAIN * read).astype(BF16)
            state = retention * state - nn(low, gram[:, lanes]) + written[:, lanes]
        state_scr[h] = state


def mixer_forward(meta, fmeta, qkv, spans):
    total, own = qkv.shape[1:]
    blocks = total // BLOCK
    stretches = BLOCK // STRETCH
    row_block = pl.BlockSpec((BLOCK, own), lambda b, *_: (b, 0))
    return pl.pallas_call(
        functools.partial(mixer_forward_kernel, spans),
        grid_spec=pltpu.PrefetchScalarGridSpec(
            num_scalar_prefetch=2,
            grid=(blocks,),
            in_specs=[whole(*qkv.shape)],
            out_specs=[
                row_block,
                row_block,
                pl.BlockSpec((1, 8, BLOCK), lambda b, *_: (b, 0, 0)),
                pl.BlockSpec(
                    (stretches, 2, HEAD_DIM, HEAD_DIM), lambda b, *_: (b, 0, 0, 0)
                ),
            ],
            scratch_shapes=[pltpu.VMEM((2, HEAD_DIM, HEAD_DIM), F32)],
        ),
        out_shape=[
            jax.ShapeDtypeStruct((total, own), BF16),
            jax.ShapeDtypeStruct((total, own), F32),
            jax.ShapeDtypeStruct((blocks, 8, BLOCK), F32),
            jax.ShapeDtypeStruct((blocks * stretches, 2, HEAD_DIM, HEAD_DIM), BF16),
        ],
        compiler_params=params(),
        cost_estimate=cost(4e9, 12e6),
        name="mixer_forward",
    )(meta, fmeta, qkv)


def mixer_backward_kernel(
    spans,
    blocks,
    meta,
    fmeta,
    qkv,
    grad_out,
    attended,
    log_total,
    states,
    grads,
    key_t,
    key_sum,
    value_sum,
    query_t,
    state_grad,
):
    block = blocks - 1 - pl.program_id(0)
    first_row = block * BLOCK
    start_two, start_three = meta[0], meta[1]
    row = first_row + lax.broadcasted_iota(jnp.int32, (1, BLOCK), 1)
    begin = jnp.where(row >= start_three, start_three, jnp.where(row >= start_two, start_two, 0))
    first_begin = jnp.where(
        first_row >= start_three, start_three, jnp.where(first_row >= start_two, start_two, 0)
    )
    scale = HEAD_DIM ** (-0.5)
    factor = scale * LOG2E
    stretches = BLOCK // STRETCH
    here = pl.ds(pl.multiple_of(first_row, BLOCK), BLOCK)

    @pl.when(pl.program_id(0) == 0)
    def _():
        key_sum[...] = jnp.zeros_like(key_sum)
        value_sum[...] = jnp.zeros_like(value_sum)
        state_grad[...] = jnp.zeros_like(state_grad)
        for h in range(2):
            for b in range(blocks):
                rows = slice(b * BLOCK, (b + 1) * BLOCK)
                key = qkv[1, rows, h * HEAD_DIM : (h + 1) * HEAD_DIM]
                key_t[h, :, rows] = key.astype(F32).T.astype(BF16)

    for h in range(2):
        cols = slice(h * HEAD_DIM, (h + 1) * HEAD_DIM)
        window = meta[5 + h]
        low_key = jnp.maximum(row - window + 1, begin)
        first_key = jnp.maximum(first_row - window + 1, first_begin)
        count = block - first_key // BLOCK + 1
        product = grad_out[:, cols].astype(F32) * attended[:, cols]
        inner = nt(jnp.ones((8, HEAD_DIM), F32), product, lax.Precision.HIGHEST)[0:1]
        logs = log_total[0, h : h + 1, :]

        def attend(span, cols=cols, low_key=low_key, h=h, inner=inner, logs=logs):
            start = pl.multiple_of(jnp.maximum(first_row + BLOCK - span, 0), BLOCK)
            there = pl.ds(start, span)
            query = qkv[0, here, cols]
            grad = grad_out[:, cols]
            score = nt(qkv[1, there, cols], query)
            position = start + lax.broadcasted_iota(jnp.int32, (span, BLOCK), 0)
            allowed = (position >= low_key) & (position <= row)
            weight = jnp.where(allowed, jnp.exp2(score * factor - logs), 0.0)
            grad_weight = nt(qkv[2, there, cols], grad)
            grad_score = (weight * (grad_weight - inner)).astype(BF16)
            value_sum[h, there, :] += nn(weight.astype(BF16), grad)
            key_sum[h, there, :] += nn(grad_score, query)
            query_t[h] = nn(key_t[h, :, there], grad_score)

        span_variants(count, spans, attend)

    for h in range(2):
        cols = slice(h * HEAD_DIM, (h + 1) * HEAD_DIM)
        query_unit, query_inverse = unit_rows(qkv[0, here, cols].astype(F32))
        key_unit, key_inverse = unit_rows(qkv[1, here, cols].astype(F32))
        value = qkv[2, here, cols].astype(F32)
        key_low = key_unit.astype(BF16)
        grad = grad_out[:, cols]
        retention, step_size = fmeta[h], fmeta[2 + h]
        gram = (
            nn(key_unit.T.astype(BF16), stretch_columns(key_low, stretches)) * step_size
        ).astype(BF16)
        read_grad = MEMORY_GAIN * nn(
            grad.astype(F32).T.astype(BF16),
            stretch_columns(query_unit.astype(BF16), stretches),
        )
        carried = state_grad[h]
        query_grads, key_grads, value_grads = [], [], []
        for n in reversed(range(stretches)):
            row_at = first_row + n * STRETCH
            keep = jnp.where((row_at == start_two) | (row_at == start_three), 0.0, 1.0)
            rows = slice(n * STRETCH, (n + 1) * STRETCH)
            lanes = slice(n * HEAD_DIM, (n + 1) * HEAD_DIM)
            carried_low = carried.astype(BF16)
            state = states[n, h]
            key_rows = key_low[rows]
            pulled = nt(key_rows, carried_low)
            error = nt(key_rows, state) - value[rows]
            value_grads.append(step_size * pulled)
            key_grads.append(
                -step_size
                * (nn(pulled.astype(BF16), state) + nn(error.astype(BF16), carried_low))
            )
            query_grads.append(MEMORY_GAIN * nn(grad[rows], state))
            carried = keep * (
                read_grad[:, lanes] + retention * carried - nn(carried_low, gram[:, lanes])
            )
        state_grad[h] = carried
        query_unit_grad = jnp.concatenate(query_grads[::-1], 0)
        key_unit_grad = jnp.concatenate(key_grads[::-1], 0)
        value_grad = jnp.concatenate(value_grads[::-1], 0)
        query_memory = query_inverse * (
            query_unit_grad
            - query_unit * jnp.sum(query_unit * query_unit_grad, -1, keepdims=True)
        )
        key_memory = key_inverse * (
            key_unit_grad - key_unit * jnp.sum(key_unit * key_unit_grad, -1, keepdims=True)
        )
        grads[0, :, cols] = (scale * query_t[h].T + query_memory).astype(BF16)
        grads[1, :, cols] = (scale * key_sum[h, here, :] + key_memory).astype(BF16)
        grads[2, :, cols] = (value_sum[h, here, :] + value_grad).astype(BF16)


def mixer_backward(meta, fmeta, qkv, grad_pieces, attended, log_total, states, spans):
    total, own = qkv.shape[1:]
    blocks = total // BLOCK
    stretches = BLOCK // STRETCH
    per_piece = grad_pieces.shape[1] // BLOCK

    def piece_at(step, meta, fmeta):
        block = blocks - 1 - step
        return ((block // per_piece) ^ meta[7], block % per_piece, 0)

    row_block = pl.BlockSpec((BLOCK, own), lambda s, *_: (blocks - 1 - s, 0))
    return pl.pallas_call(
        functools.partial(mixer_backward_kernel, spans, blocks),
        grid_spec=pltpu.PrefetchScalarGridSpec(
            num_scalar_prefetch=2,
            grid=(blocks,),
            in_specs=[
                whole(*qkv.shape),
                pl.BlockSpec((None, BLOCK, own), piece_at),
                row_block,
                pl.BlockSpec((1, 8, BLOCK), lambda s, *_: (blocks - 1 - s, 0, 0)),
                pl.BlockSpec(
                    (stretches, 2, HEAD_DIM, HEAD_DIM), lambda s, *_: (blocks - 1 - s, 0, 0, 0)
                ),
            ],
            out_specs=pl.BlockSpec((3, BLOCK, own), lambda s, *_: (0, blocks - 1 - s, 0)),
            scratch_shapes=[
                pltpu.VMEM((2, HEAD_DIM, total), BF16),
                pltpu.VMEM((2, total, HEAD_DIM), F32),
                pltpu.VMEM((2, total, HEAD_DIM), F32),
                pltpu.VMEM((2, HEAD_DIM, BLOCK), F32),
                pltpu.VMEM((2, HEAD_DIM, HEAD_DIM), F32),
            ],
        ),
        out_shape=jax.ShapeDtypeStruct(qkv.shape, BF16),
        compiler_params=params(),
        cost_estimate=cost(10e9, 16e6),
        name="mixer_backward",
    )(meta, fmeta, qkv, grad_pieces, attended, log_total, states)


def out_forward_kernel(meta, mine, other, weight_t, lower, upper_t, branch, latent):
    own = mine.shape[1]
    select = adapter_select(meta, meta[8], mine.shape[0], 1)
    lat = keep_low(select, nn(mine[...], lower[:own]) + nn(other[...], lower[own:]))
    latent[...] = lat
    branch[...] = (
        nt(mine[...], weight_t[:, :own])
        + nt(other[...], weight_t[:, own:])
        + nt(lat, upper_t[...])
    ).astype(BF16)


def out_forward(meta, mine, other, weight_t, lower, upper_t):
    rows, own = mine.shape
    width = weight_t.shape[0]
    return pl.pallas_call(
        out_forward_kernel,
        grid_spec=pltpu.PrefetchScalarGridSpec(
            num_scalar_prefetch=1,
            grid=(1,),
            in_specs=[
                whole(rows, own),
                whole(rows, own),
                whole(*weight_t.shape),
                whole(*lower.shape),
                whole(*upper_t.shape),
            ],
            out_specs=[whole(rows, width), whole(rows, LANES)],
        ),
        out_shape=[
            jax.ShapeDtypeStruct((rows, width), BF16),
            jax.ShapeDtypeStruct((rows, LANES), BF16),
        ],
        compiler_params=params(),
        cost_estimate=cost(2 * rows * width * 640, 5e6),
        name="out_forward",
    )(meta, mine, other, weight_t, lower, upper_t)


def out_backward_kernel(meta, grad, weight_t, lower, upper_t, mine, other, latent_grad):
    own = mine.shape[1]
    select = adapter_select(meta, meta[8], mine.shape[0], 1)
    lat = keep_low(select, nn(grad[...], upper_t[...]))
    latent_grad[...] = lat
    mine[...] = (nn(grad[...], weight_t[:, :own]) + nt(lat, lower[:own])).astype(BF16)
    other[...] = (nn(grad[...], weight_t[:, own:]) + nt(lat, lower[own:])).astype(BF16)


def out_backward(meta, grad, weight_t, lower, upper_t):
    rows, width = grad.shape
    own = weight_t.shape[1] // 2
    return pl.pallas_call(
        out_backward_kernel,
        grid_spec=pltpu.PrefetchScalarGridSpec(
            num_scalar_prefetch=1,
            grid=(1,),
            in_specs=[
                whole(rows, width),
                whole(*weight_t.shape),
                whole(*lower.shape),
                whole(*upper_t.shape),
            ],
            out_specs=[whole(rows, own), whole(rows, own), whole(rows, LANES)],
        ),
        out_shape=[
            jax.ShapeDtypeStruct((rows, own), BF16),
            jax.ShapeDtypeStruct((rows, own), BF16),
            jax.ShapeDtypeStruct((rows, LANES), BF16),
        ],
        compiler_params=params(),
        cost_estimate=cost(2 * rows * width * 640, 5e6),
        name="out_backward",
    )(meta, grad, weight_t, lower, upper_t)


def ffn_kernel(
    first,
    meta,
    x0,
    x1,
    g0,
    g1,
    weight,
    lower,
    upper_t,
    down_lower,
    down_upper_t,
    dx0,
    dx1,
    swiglu,
    gate_grad,
    up_grad,
    latent,
    latent_grad,
    down_latent_grad,
    x_scr,
    g_scr,
    dx_scr,
):
    step = pl.program_id(0)
    rows = x_scr.shape[0]
    halves = x0.shape[0] // rows
    piece, part = step // halves, step % halves
    at = pl.ds(pl.multiple_of(part * rows, rows), rows)
    for k, (x_ref, g_ref) in enumerate(((x0, g0), (x1, g1))):

        @pl.when(piece == k)
        def _():
            x_scr[...] = x_ref[at, :]
            g_scr[...] = g_ref[at, :]

    first_row = (meta[7] ^ (first + piece)) * (rows * halves) + part * rows
    select = adapter_select(meta, first_row, rows, 2)
    select_one = select[:, :LANES]
    x = x_scr[...]
    grad = g_scr[...]
    lat = keep_low(select, nn(x, lower[...]))
    latent[...] = lat
    gate = nn(x, weight[0]) + nt(lat[:, :LANES], upper_t[0])
    up = nn(x, weight[1]) + nt(lat[:, LANES:], upper_t[1])
    sigmoid = 1.0 / (1.0 + jnp.exp(-gate))
    silu = gate * sigmoid
    swiglu[...] = (silu * up).astype(BF16)
    down_lat = keep_low(select_one, nn(grad, down_upper_t[...]))
    down_latent_grad[...] = down_lat
    wide_grad = nn(grad, weight[2]) + nt(down_lat, down_lower[...])
    d_up = (wide_grad * silu).astype(BF16)
    d_gate = (wide_grad * up * (sigmoid * (1.0 + gate * (1.0 - sigmoid)))).astype(BF16)
    gate_grad[...] = d_gate
    up_grad[...] = d_up
    lat_grad = keep_low(
        select, jnp.concatenate([nn(d_gate, upper_t[0]), nn(d_up, upper_t[1])], 1)
    )
    latent_grad[...] = lat_grad
    dx_scr[...] = (
        nt(d_gate, weight[0]) + nt(d_up, weight[1]) + nt(lat_grad, lower[...])
    ).astype(BF16)
    for k, dx_ref in enumerate((dx0, dx1)):

        @pl.when(piece == k)
        def _():
            dx_ref[at, :] = dx_scr[...]


def ffn(meta, first, xs, grads, weight, lower, upper_t, down_lower, down_upper_t):
    rows, width = xs[0].shape
    hidden = weight.shape[2]
    total = 2 * rows
    grid = total // BLOCK
    block = lambda columns: pl.BlockSpec((BLOCK, columns), lambda s, *_: (s, 0))
    return pl.pallas_call(
        functools.partial(ffn_kernel, first),
        grid_spec=pltpu.PrefetchScalarGridSpec(
            num_scalar_prefetch=1,
            grid=(grid,),
            in_specs=[whole(rows, width)] * 4
            + [
                whole(*weight.shape),
                whole(*lower.shape),
                whole(*upper_t.shape),
                whole(*down_lower.shape),
                whole(*down_upper_t.shape),
            ],
            out_specs=[whole(rows, width)] * 2
            + [block(hidden)] * 3
            + [block(2 * LANES), block(2 * LANES), block(LANES)],
            scratch_shapes=[pltpu.VMEM((BLOCK, width), BF16)] * 3,
        ),
        out_shape=[jax.ShapeDtypeStruct((rows, width), BF16)] * 2
        + [jax.ShapeDtypeStruct((total, hidden), BF16)] * 3
        + [
            jax.ShapeDtypeStruct((total, 2 * LANES), BF16),
            jax.ShapeDtypeStruct((total, 2 * LANES), BF16),
            jax.ShapeDtypeStruct((total, LANES), BF16),
        ],
        compiler_params=params(),
        cost_estimate=cost(2 * total * width * hidden * 6.0, 14e6),
        name="ffn",
    )(meta, *xs, *grads, weight, lower, upper_t, down_lower, down_upper_t)


def down_kernel(meta, first, rows_each, sw, weight, lower, upper_t, y, latent):
    step = pl.program_id(0)
    rows = sw.shape[0]
    per = rows_each // rows
    first_row = (meta[7] ^ (first + step // per)) * rows_each + (step % per) * rows
    select = adapter_select(meta, first_row, rows, 1)
    lat = keep_low(select, nn(sw[...], lower[...]))
    latent[...] = lat
    y[...] = (nt(sw[...], weight[...]) + nt(lat, upper_t[...])).astype(BF16)


def down(meta, first, rows_each, sw, weight, lower, upper_t):
    total, hidden = sw.shape
    width = weight.shape[1]
    return pl.pallas_call(
        lambda meta, *refs: down_kernel(meta, first, rows_each, *refs),
        grid_spec=pltpu.PrefetchScalarGridSpec(
            num_scalar_prefetch=1,
            grid=(total // BLOCK,),
            in_specs=[
                pl.BlockSpec((BLOCK, hidden), lambda s, *_: (s, 0)),
                pl.BlockSpec((None, width, hidden), lambda s, *_: (2, 0, 0), pipeline_mode=pl.Buffered(1)),
                whole(*lower.shape),
                whole(*upper_t.shape),
            ],
            out_specs=[
                pl.BlockSpec((BLOCK, width), lambda s, *_: (s, 0)),
                pl.BlockSpec((BLOCK, LANES), lambda s, *_: (s, 0)),
            ],
        ),
        out_shape=[
            jax.ShapeDtypeStruct((total, width), BF16),
            jax.ShapeDtypeStruct((total, LANES), BF16),
        ],
        compiler_params=params(),
        cost_estimate=cost(2 * total * width * hidden * 1.3, 8e6),
        name="down",
    )(meta, sw, weight, lower, upper_t)


def pair_kernel(count, steps, *refs):
    lefts, rights = refs[:count], refs[count : 2 * count]
    outs, sums = refs[2 * count : 3 * count], refs[3 * count :]
    step = pl.program_id(0)
    for left, right, out, total in zip(lefts, rights, outs, sums):
        a, b = left.shape[1], right.shape[1]

        @pl.when(step == 0)
        def _():
            total[...] = jnp.zeros_like(total)

        total[:, :b] += tn(left[...], right[...])

        @pl.when(step == steps - 1)
        def _():
            out[...] = total[...].T[:b].astype(BF16)


def pair_sums(pairs, rows=512):
    count = len(pairs)
    total = pairs[0][0].shape[0]
    rows = min(rows, total)
    steps = total // rows
    lefts, rights = [p[0] for p in pairs], [p[1] for p in pairs]
    flops = sum(2 * total * l.shape[1] * r.shape[1] for l, r in pairs)
    padded = lambda n: -(-n // LANES) * LANES
    return pl.pallas_call(
        functools.partial(pair_kernel, count, steps),
        grid=(steps,),
        in_specs=[pl.BlockSpec((rows, v.shape[1]), lambda s: (s, 0)) for v in lefts + rights],
        out_specs=[whole(r.shape[1], l.shape[1]) for l, r in pairs],
        out_shape=[jax.ShapeDtypeStruct((r.shape[1], l.shape[1]), BF16) for l, r in pairs],
        scratch_shapes=[pltpu.VMEM((l.shape[1], padded(r.shape[1])), F32) for l, r in pairs],
        compiler_params=params(),
        cost_estimate=cost(flops * 2, 10e6),
        name="pair_sums",
    )(*lefts, *rights)


def qkv_backward_kernel(meta, first, grads, weight, lower, upper_t, dx):
    step = pl.program_id(0)
    rows = dx.shape[0]
    halves = 2
    first_row = (meta[7] ^ first) * (halves * rows) + step * rows
    select = adapter_select(meta, first_row, rows, 3)
    lat = keep_low(
        select, jnp.concatenate([nn(grads[m], upper_t[m]) for m in range(3)], 1)
    )
    total = nt(lat, lower[...])
    for m in range(3):
        total += nt(grads[m], weight[m])
    dx[...] = total.astype(BF16)


def qkv_backward(meta, first, rows, grads, weight, lower, upper_t):
    own = grads.shape[2]
    width = lower.shape[0]
    part = rows // 2
    return pl.pallas_call(
        lambda meta, *refs: qkv_backward_kernel(meta, first, *refs),
        grid_spec=pltpu.PrefetchScalarGridSpec(
            num_scalar_prefetch=1,
            grid=(2,),
            in_specs=[
                pl.BlockSpec((3, part, own), lambda s, meta: (0, (meta[7] ^ first) * 2 + s, 0)),
                whole(*weight.shape),
                whole(*lower.shape),
                whole(*upper_t.shape),
            ],
            out_specs=pl.BlockSpec((part, width), lambda s, *_: (s, 0)),
        ),
        out_shape=jax.ShapeDtypeStruct((rows, width), BF16),
        compiler_params=params(),
        cost_estimate=cost(2 * rows * width * 1250, 5e6),
        name="qkv_backward",
    )(meta, grads, weight, lower, upper_t)


def qkv_pairs_kernel(steps, meta, normed, latent, grads, upper_t, lower_out, upper_out, low_sum, up_sum):
    step = pl.program_id(0)
    rows = normed.shape[0]
    select = adapter_select(meta, step * rows, rows, 3)
    lat = keep_low(
        select, jnp.concatenate([nn(grads[m], upper_t[m]) for m in range(3)], 1)
    )

    @pl.when(step == 0)
    def _():
        low_sum[...] = jnp.zeros_like(low_sum)
        up_sum[...] = jnp.zeros_like(up_sum)

    low_sum[...] += tn(lat, normed[...])
    for m in range(3):
        up_sum[m] += tn(latent[:, m * LANES : (m + 1) * LANES], grads[m])

    @pl.when(step == steps - 1)
    def _():
        lower_out[...] = low_sum[...].T.astype(BF16)
        for m in range(3):
            upper_out[m] = up_sum[m].T.astype(BF16)


def qkv_pairs(meta, normed, latent, grads, upper_t):
    total, width = normed.shape
    own = grads.shape[2]
    rows = 512
    steps = total // rows
    return pl.pallas_call(
        functools.partial(qkv_pairs_kernel, steps),
        grid_spec=pltpu.PrefetchScalarGridSpec(
            num_scalar_prefetch=1,
            grid=(steps,),
            in_specs=[
                pl.BlockSpec((rows, width), lambda s, *_: (s, 0)),
                pl.BlockSpec((rows, 3 * LANES), lambda s, *_: (s, 0)),
                pl.BlockSpec((3, rows, own), lambda s, *_: (0, s, 0)),
                whole(*upper_t.shape),
            ],
            out_specs=[whole(width, 3 * LANES), whole(3, own, LANES)],
            scratch_shapes=[
                pltpu.VMEM((3 * LANES, width), F32),
                pltpu.VMEM((3, LANES, own), F32),
            ],
        ),
        out_shape=[
            jax.ShapeDtypeStruct((width, 3 * LANES), BF16),
            jax.ShapeDtypeStruct((3, own, LANES), BF16),
        ],
        compiler_params=params(),
        cost_estimate=cost(2 * total * width * 3 * LANES * 2, 10e6),
        name="qkv_pairs",
    )(meta, normed, latent, grads, upper_t)


def swap(values, bit):
    size = lax.axis_size("tensor")
    return lax.ppermute(values, "tensor", [(i, i ^ bit) for i in range(size)])


def swap_dp(values, bits):
    size = lax.axis_size("dp")
    return lax.ppermute(values, "dp", [(i, i ^ bits) for i in range(size)])


def gather_tensor(values):
    far = swap(values, 2)
    return [values, swap(values, 1), far, swap(far, 1)]


def tensor_order(pieces, place):
    stacked = jnp.stack(pieces)
    for bit in (1, 2):
        moved = stacked.reshape((2, 2) + pieces[0].shape)[:, ::-1] if bit == 1 else (
            stacked.reshape((2, 2) + pieces[0].shape)[::-1]
        )
        stacked = jnp.where((place & bit) != 0, moved.reshape(stacked.shape), stacked)
    return stacked


def gather_dp(values):
    size = lax.axis_size("dp")
    if size != 8:
        return lax.all_gather(values, "dp", axis=0, tiled=False)
    place = lax.axis_index("dp")
    near = [values] + [swap_dp(values, 2 * k) for k in (1, 2, 3)]
    result = jnp.zeros((size,) + values.shape, values.dtype)
    for k, piece in enumerate(near):
        result = lax.dynamic_update_index_in_dim(result, piece, place ^ (2 * k), 0)
        result = lax.dynamic_update_index_in_dim(result, swap_dp(piece, 1), place ^ (2 * k + 1), 0)
    return result


def exchange_dp(values):
    return lax.all_to_all(values, "dp", split_axis=0, concat_axis=0, tiled=True)


def norm_gradient(values, gain, grad):
    inverse = lax.rsqrt(jnp.mean(values * values, -1, keepdims=True) + EPSILON)
    scaled = gain * grad
    return inverse * scaled - values * (
        inverse * inverse * inverse * jnp.mean(scaled * values, -1, keepdims=True)
    )


def after(values, *earlier):
    return lax.optimization_barrier((values,) + earlier)[0]


def per_device(
    tokens,
    cotangent,
    attention_gain,
    feedforward_gain,
    query_key_value_matrix,
    output_matrix,
    feedforward_matrix,
    down_matrix,
    memory_retention,
    memory_step_size,
    sequence_length,
    sequence_permutation,
    sequence_adapter,
    head_span_window,
    query_key_value_lower,
    query_key_value_upper,
    output_adapter_lower,
    output_adapter_upper,
    feedforward_adapter_lower,
    feedforward_adapter_upper,
    down_adapter_lower,
    down_adapter_upper,
):
    groups = lax.axis_size("dp")
    group = lax.axis_index("dp")
    place = lax.axis_index("tensor")
    quarter, width = tokens.shape
    slot = quarter // groups
    heads_own = query_key_value_matrix.shape[2]
    hidden = feedforward_matrix.shape[2]

    members = lax.dynamic_slice_in_dim(sequence_permutation, group * SEQ_G, SEQ_G)
    hits = members[:, None] == jnp.arange(sequence_length.shape[0], dtype=jnp.int32)[None, :]
    lengths = jnp.sum(jnp.where(hits, sequence_length[None, :], 0), 1)
    adapters = jnp.sum(jnp.where(hits, sequence_adapter[None, :], 0), 1)
    head_at = place * 2
    windows = lax.dynamic_slice_in_dim(head_span_window, head_at, 2)
    meta = jnp.concatenate(
        [
            jnp.stack([lengths[0], lengths[0] + lengths[1]]),
            adapters,
            windows,
            jnp.stack([place, jnp.int32(0)]),
        ]
    ).astype(jnp.int32)
    at_piece = lambda k: meta.at[8].set((place ^ k) * quarter)
    fmeta = jnp.concatenate(
        [
            lax.dynamic_slice_in_dim(memory_retention, head_at, 2),
            lax.dynamic_slice_in_dim(memory_step_size, head_at, 2) / STRETCH,
        ]
    )
    spans = (2, 3, 4, 5)

    arrived = exchange_dp(tokens.reshape(groups, slot, width)).reshape(quarter, width)
    token_pieces = gather_tensor(arrived)

    def own_upper(values):
        return jnp.swapaxes(values, -1, -2)

    axes = ("dp", "tensor")
    tensors = lax.axis_size("tensor")
    to_user = [(j, (j % groups) * tensors + j // groups) for j in range(groups * tensors)]
    to_owner = [(b, a) for a, b in to_user]

    def flat(parts):
        return jnp.concatenate([v.reshape(-1, LANES) for v in parts], 0)

    def unflat(values, shapes):
        out, at = [], 0
        for shape in shapes:
            size = 1
            for n in shape[:-1]:
                size *= n
            out.append(lax.slice_in_dim(values, at, at + size, axis=values.ndim - 2).reshape(values.shape[:-2] + shape))
            at += size
        return out

    share = query_key_value_lower.shape[1]
    up_share = feedforward_adapter_upper.shape[2]
    qkv_upper_own = lax.ppermute(own_upper(query_key_value_upper), axes, to_user)
    qkv_lower_all = tensor_order(gather_tensor(query_key_value_lower), place)
    qkv_lower_all = jnp.swapaxes(qkv_lower_all, 0, 1).reshape(3, tensors * share, LANES)
    qkv_pack = gather_dp(flat([qkv_lower_all, qkv_upper_own]))
    qkv_a, qkv_b = unflat(qkv_pack, [(3, tensors * share, LANES), (3, share, LANES)])
    qkv_a = jnp.moveaxis(qkv_a, 1, 2).reshape(width, 3 * LANES)
    qkv_b = jnp.moveaxis(qkv_b, 0, 1).reshape(3, heads_own, LANES)
    qkv_w = jnp.moveaxis(gather_dp(query_key_value_matrix), 0, 1).reshape(3, width, heads_own)

    cot_arrived = exchange_dp(
        after(cotangent, token_pieces[3]).reshape(groups, slot, width)
    ).reshape(quarter, width)
    grad_pieces = gather_tensor(cot_arrived)
    out_t = output_matrix.T
    ffn_pack = jnp.concatenate([feedforward_matrix, down_matrix.T[None]], 0)
    ffn_w = jnp.moveaxis(lax.all_gather(ffn_pack, "dp", axis=0, tiled=False), 0, 1).reshape(3, width, hidden)
    out_pair = jnp.concatenate([out_t, swap(out_t, 2)], 1)
    out_w = gather_dp(out_pair).reshape(width, 2 * heads_own)
    full_shapes = [(2, share, LANES), (share, LANES), (share, LANES)]
    full = tensor_order(
        gather_tensor(
            flat([feedforward_adapter_lower, output_adapter_upper.T, down_adapter_upper.T])
        ),
        place,
    )
    ffn_a, out_b, down_b = unflat(full, full_shapes)
    user = lax.ppermute(
        flat([own_upper(feedforward_adapter_upper), down_adapter_lower, output_adapter_lower]),
        axes,
        to_user,
    )
    ffn_b, down_a, out_a = unflat(user, [(2, up_share, LANES), (up_share, LANES), (share, LANES)])
    late_shapes = [
        (2, tensors * share, LANES),
        (tensors * share, LANES),
        (tensors * share, LANES),
        (2, up_share, LANES),
        (up_share, LANES),
        (share, LANES),
        (share, LANES),
    ]
    late = lax.all_gather(
        flat([jnp.swapaxes(ffn_a, 0, 1), out_b, down_b, ffn_b, down_a, out_a, swap(out_a, 2)]),
        "dp",
        axis=0,
        tiled=False,
    )
    ffn_a, out_b, down_b, ffn_b, down_a, out_a, out_a_far = unflat(late, late_shapes)
    ffn_a = jnp.moveaxis(ffn_a, 1, 2).reshape(width, 2 * LANES)
    out_b = out_b.reshape(width, LANES)
    down_b = down_b.reshape(width, LANES)
    ffn_b = jnp.moveaxis(ffn_b, 0, 1).reshape(2, hidden, LANES)
    down_a = down_a.reshape(hidden, LANES)
    out_a = jnp.concatenate([out_a.reshape(heads_own, LANES), out_a_far.reshape(heads_own, LANES)], 0)

    gain_one = attention_gain.reshape(1, width)
    gain_two = feedforward_gain.reshape(1, width)
    normed, qkv, qkv_latent = project_qkv(meta, token_pieces, gain_one, qkv_w, qkv_a, qkv_b)
    heads, attended, log_total, states = mixer_forward(meta, fmeta, qkv, spans)
    half = 2 * quarter
    chip = place // 2
    heads_far = swap(lax.dynamic_slice_in_dim(heads, (1 - chip) * half, half, 0), 2)
    rows_of = lambda values, k: lax.dynamic_slice_in_dim(values, (place ^ k) * quarter, quarter, 0)
    rows_far = lambda k: lax.dynamic_slice_in_dim(heads_far, ((place ^ k) % 2) * quarter, quarter, 0)
    heads_mine = [rows_of(heads, k) for k in (0, 1)]
    heads_other = [rows_far(k) for k in (0, 1)]
    branch_mate, out_latent_mate = out_forward(at_piece(1), heads_mine[1], heads_other[1], out_w, out_a, out_b)
    branch_got = swap(branch_mate, 1)
    branch_own, out_latent_own = out_forward(at_piece(0), heads_mine[0], heads_other[0], out_w, out_a, out_b)
    stream = arrived.astype(F32)
    hidden_one = stream + (branch_own.astype(F32) + branch_got.astype(F32))
    normed_two = (
        hidden_one
        * lax.rsqrt(jnp.mean(hidden_one * hidden_one, -1, keepdims=True) + EPSILON)
        * gain_two
    ).astype(BF16)
    two = gather_tensor(normed_two)

    near = ffn(meta, 0, two[:2], grad_pieces[:2], ffn_w, ffn_a, ffn_b, down_a, down_b)
    far = ffn(meta, 2, two[2:], grad_pieces[2:], ffn_w, ffn_a, ffn_b, down_a, down_b)

    def scatter(own, mate, far_mate, across):
        onward = (far_mate.astype(F32) + swap(across, 1).astype(F32)).astype(BF16)
        return own.astype(F32) + swap(mate, 1).astype(F32) + swap(onward, 2).astype(F32)

    grad_two = scatter(near[0], near[1], far[0], far[1])
    grad_out = cot_arrived.astype(F32)
    grad_one = grad_out + norm_gradient(hidden_one, gain_two, grad_two)
    grad_one_low = grad_one.astype(BF16)

    y_near, down_latent_near = down(meta, 0, quarter, near[2], ffn_w, down_a, down_b)
    y_far, down_latent_far = down(meta, 2, quarter, far[2], ffn_w, down_a, down_b)
    ffn_branch = scatter(y_near[:quarter], y_near[quarter:], y_far[:quarter], y_far[quarter:])
    mixed_rows = (hidden_one + ffn_branch).astype(BF16)
    mixed = exchange_dp(mixed_rows.reshape(groups, slot, width)).reshape(quarter, width)
    ffn_terms = []
    for part, down_latent, x, grad in (
        (near, down_latent_near, two[:2], grad_pieces[:2]),
        (far, down_latent_far, two[2:], grad_pieces[2:]),
    ):
        _, _, sw, d_gate, d_up, lat, lat_grad, down_lat_grad = part
        ffn_terms.append(
            pair_sums(
                [
                    (lat_grad, jnp.concatenate(x, 0)),
                    (lat[:, :LANES], d_gate),
                    (lat[:, LANES:], d_up),
                    (down_lat_grad, sw),
                    (down_latent, jnp.concatenate(grad, 0)),
                ]
            )
        )
    ffn_terms = [(a.astype(F32) + b.astype(F32)).astype(BF16) for a, b in zip(*ffn_terms)]

    grad_mate = swap(grad_one_low, 1)
    back_own = out_backward(at_piece(0), grad_one_low, out_w, out_a, out_b)
    back_mate = out_backward(at_piece(1), grad_mate, out_w, out_a, out_b)
    got_own, got_mate = swap(back_own[1], 2), swap(back_mate[1], 2)
    heads_grad = jnp.stack([back_own[0], back_mate[0], got_own, got_mate])
    qkv_grads = mixer_backward(meta, fmeta, qkv, heads_grad, attended, log_total, states, spans)
    out_terms = pair_sums(
        [
            (jnp.concatenate([back_own[2], back_mate[2]], 0), jnp.concatenate([jnp.concatenate([heads_mine[0], heads_other[0]], 1), jnp.concatenate([heads_mine[1], heads_other[1]], 1)], 0)),
            (jnp.concatenate([out_latent_own, out_latent_mate], 0), jnp.concatenate([grad_one_low, grad_mate], 0)),
        ]
    )

    terms = [qkv_backward(meta, k, quarter, qkv_grads, qkv_w, qkv_a, qkv_b) for k in (3, 2, 1, 0)][::-1]
    grad_normed = scatter(*terms)
    qkv_lower_term, qkv_upper_term = qkv_pairs(meta, normed, qkv_latent, qkv_grads, qkv_b)
    grad_input = (grad_one + norm_gradient(stream, gain_one, grad_normed)).astype(BF16)
    token_grad = exchange_dp(grad_input.reshape(groups, slot, width)).reshape(quarter, width)

    def reduce_terms(full_terms, own_terms, own_far):
        columns = sum(v.shape[1] for v in full_terms)
        wide = jnp.concatenate(full_terms, 1).reshape(groups, tensors, share, columns)
        by_rel = lambda k: lax.dynamic_index_in_dim(wide, place ^ k, 1, keepdims=False)
        wide = scatter(by_rel(0), by_rel(1), by_rel(2), by_rel(3)).astype(BF16)
        parts = [wide[:, :, i * LANES : (i + 1) * LANES] for i in range(columns // LANES)]
        if own_far is not None:
            mine, other = own_far
            own_terms = own_terms + [(mine.astype(F32) + swap(other, 2).astype(F32)).astype(BF16)]
        pack = jnp.concatenate(parts + own_terms, 1)
        summed = jnp.sum(exchange_dp(pack).astype(F32), 0)
        cut = share * len(parts)
        own = lax.ppermute(summed[cut:], axes, to_owner)
        return summed[:cut].reshape(len(parts), share, LANES), own

    ffn_full, ffn_own = reduce_terms(
        [ffn_terms[0], out_terms[1], ffn_terms[4]],
        [
            ffn_terms[1].reshape(groups, up_share, LANES),
            ffn_terms[2].reshape(groups, up_share, LANES),
            ffn_terms[3].reshape(groups, up_share, LANES),
        ],
        [v.reshape(groups, share, LANES) for v in (out_terms[0][:heads_own], out_terms[0][heads_own:])],
    )
    qkv_full, qkv_own = reduce_terms(
        [qkv_lower_term],
        [jnp.moveaxis(qkv_upper_term.reshape(3, groups, share, LANES), 1, 0).reshape(groups, 3 * share, LANES)],
        None,
    )
    ffn_own_parts = [ffn_own[i * up_share : (i + 1) * up_share] for i in range(3)]
    return (
        mixed,
        token_grad,
        qkv_full,
        jnp.swapaxes(qkv_own.reshape(3, share, LANES), 1, 2),
        ffn_own[3 * up_share :],
        ffn_full[2].T,
        ffn_full[:2],
        jnp.stack([ffn_own_parts[0].T, ffn_own_parts[1].T]),
        ffn_own_parts[2],
        ffn_full[3].T,
    )


def solution(mesh):
    both = ("dp", "tensor")
    rows = P(both, None)
    lower = P(None, both, None)
    upper = P(None, None, both)
    return jax.shard_map(
        per_device,
        mesh=mesh,
        in_specs=(
            rows,
            rows,
            P(),
            P(),
            P(None, "dp", "tensor"),
            P("tensor", "dp"),
            P(None, "dp", "tensor"),
            P("tensor", "dp"),
            P(),
            P(),
            P(),
            P(),
            P(),
            P(),
            lower,
            upper,
            rows,
            P(None, both),
            lower,
            upper,
            rows,
            P(None, both),
        ),
        out_specs=(
            rows,
            rows,
            lower,
            upper,
            rows,
            P(None, both),
            lower,
            upper,
            rows,
            P(None, both),
        ),
        check_vma=False,
    )
```

time: 2820 us -> 682 us (0.24)
  waiting for transfers between devices: 1260 us -> 207 us
  matrix products: 694 us -> 0 us
  blocking collectives: 385 us -> 0 us
  local copies, waits for them, and re-layouts: 326 us -> 71.3 us
  Pallas kernels: 0 us -> 205 us
  starting transfers between devices: 12.3 us -> 114 us
  other arithmetic: 96.9 us -> 59.3 us
    reduce_scatter x11 -> x0, waiting for transfers between devices: 961 us -> none  [the longest x1 137 us: per_device(): lax.psum_scatter(ffn_b_term, ('dp', 'tensor'), scatter_dimension=2, tiled...]
    dot_general x404 -> x0, matrix products: 694 us -> none  [the longest x96 154 us: advance(): jnp.einsum('thd,hde->the', query_stretch, memory_state, precision=highest)]
    all_gather x8 -> x0, blocking collectives: 314 us -> none  [the longest x1 43.1 us: per_device(): lax.all_gather(down_adapter_lower, ('dp', 'tensor'), axis=0, tiled=True)]
    pallas_call x0 -> x19, Pallas kernels: none -> 205 us  [the longest x2 44.2 us: ffn(): pl.pallas_call(functools.partial(ffn_kernel, first), grid_spec=pltpu.Pref...]
    ppermute x0 -> x63, waiting for transfers between devices: none -> 185 us  [the longest x38 76.1 us: swap(): return lax.ppermute(values, 'tensor', [(i, i ^ bit) for i in range(size)])]
    unnamed x21 -> x2, waiting for transfers between devices: 137 us -> 0.03 us
    all_gather x8 -> x2, waiting for transfers between devices: 116 us -> 0.01 us  [the longest x1 0.01 us: per_device(): lax.all_gather(flat([jnp.swapaxes(ffn_a, 0, 1), out_b, down_b, ffn_b, dow...]
    dynamic_slice x104 -> x6, local copies, waits for them, and re-layouts: 94 us -> 3.12 us  [the longest x1 1.17 us: per_device(): lax.dynamic_slice_in_dim(heads, (1 - chip) * half, half, 0)]
  transfers between devices with their start and end apart: 22 -> 71, of which waited for: 16 -> 28; matrix products, arithmetic and copies ran while one was open for 4% -> 17% of each run, Pallas kernels for 0% -> 26%
where the time goes in v2:
time: 682 us; the launch traced here: 673 us
  waiting for transfers between devices  207 us (30%)
  Pallas kernels  205 us (30%)
  starting transfers between devices  114 us (17%)
  local copies, waits for them, and re-layouts  71.3 us (10%)
  other arithmetic  59.3 us (9%)
  between operations  16.6 us (2%)
    ppermute x38, waiting for transfers between devices, swap(): return lax.ppermute(values, 'tensor', [(i, i ^ bit) for i in range(size)])  76.1 us
    ppermute x21, waiting for transfers between devices, swap_dp(): return lax.ppermute(values, 'dp', [(i, i ^ bits) for i in range(size)])  74.9 us
    pallas_call x2, Pallas kernels, ffn(): pl.pallas_call(functools.partial(ffn_kernel, first), grid_spec=pltpu.Pref...  44.2 us
    ppermute x21, starting transfers between devices, swap_dp(): return lax.ppermute(values, 'dp', [(i, i ^ bits) for i in range(size)])  35 us
    ppermute x38, starting transfers between devices, swap(): return lax.ppermute(values, 'tensor', [(i, i ^ bit) for i in range(size)])  35 us
    pallas_call x1, Pallas kernels, mixer_backward(): pl.pallas_call(functools.partial(mixer_backward_kernel, spans, blocks), g...  34.2 us
    all_to_all x6, starting transfers between devices, exchange_dp(): return lax.all_to_all(values, 'dp', split_axis=0, concat_axis=0, tiled=True)  33.9 us
    ppermute x2, waiting for transfers between devices, reduce_terms(): own = lax.ppermute(summed[cut:], axes, to_owner)  32.6 us
  transfers between devices with their start and end apart: 71, of which 28 were waited for; matrix products, arithmetic and copies ran while one was open for 17% of the time, Pallas kernels for 26%

profile of v2, /device:TPU:2, one launch (start us, length us, event | category | flops | bytes accessed | tf_op | source)
XLA Modules:
  0.0 673.4 jit_solution(16898557120768663714)
XLA Ops:
  9.6 2.4 collective-permute-done.31
  12.8 4.5 collective-permute-start.33
  19.5 5.3 collective-permute-start.34
  31.3 7.1 %all-to-all-start = ((bf16[8,64,1024]{2,1,0:T(8,128)(2,1)}), bf16[8,64,1024]{2,1,0:T(8,128)(2,1)S(1)}, u32[]{:S(2)}, u32[]{:S(2)}) async-start(bf16[8,64,1024]{2,1,0:T(8,128)(2,1)} %bitcast), calls=%async_computation | async-start | bytes 2097152 | tf_op jit(solution)/shard_map/all_to_all | solution.py:799
  38.4 3.7 collective-permute-start.22
  57.1 2.4 collective-permute-start.26
  61.0 5.3 collective-permute-done.15
  72.0 2.9 collective-permute-start.6
  75.0 16.4 %collective-permute-done.26 = bf16[128,512]{0,1:T(8,128)(2,1)S(1)} collective-permute-done((bf16[128,512]{0,1:T(8,128)(2,1)}, bf16[128,512]{0,1:T(8,128)(2,1)S(1)}, u32[]{:S(2)}, u32[]{:S(2)}) %collective-permute-start.26) | collective-permute-done | bytes 131104 | tf_op jit(solution)/shard_map/ppermute | solution.py:767
  92.3 11.3 %collective-permute-start.17 = (bf16[480,128]{1,0:T(8,128)(2,1)}, bf16[480,128]{1,0:T(8,128)(2,1)}, u32[]{:S(2)}, u32[]{:S(2)}) collective-permute-start(bf16[480,128]{1,0:T(8,128)(2,1)} %pad_maximum_fusion.14), channel_id=1, source_target_pairs={{0,16},{4,20},{8,24},{12,28},{16,0},{20,4},{24,8},{28,12},{1,17},{... | collective-permute-start | bytes 368648 | tf_op jit(solution)/shard_map/ppermute | solution.py:767
  106.0 2.8 collective-permute-start.19
  108.8 27.5 %collective-permute-done.17 = bf16[480,128]{1,0:T(8,128)(2,1)} collective-permute-done((bf16[480,128]{1,0:T(8,128)(2,1)}, bf16[480,128]{1,0:T(8,128)(2,1)}, u32[]{:S(2)}, u32[]{:S(2)}) %collective-permute-start.17) | collective-permute-done | bytes 122912 | tf_op jit(solution)/shard_map/ppermute | solution.py:767
  139.8 2.9 collective-permute-done.16
  146.7 2.3 collective-permute-start.1
  151.9 5.6 collective-permute-done.25
  173.0 4.3 collective-permute-done.5
  179.2 6.0 collective-permute-done.7
  186.2 3.4 collective-permute-done.9
  191.5 13.9 %project_qkv.1 = (bf16[2048,1024]{1,0:T(8,128)(2,1)}, bf16[3,2048,256]{2,1,0:T(8,128)(2,1)}, bf16[2048,384]{1,0:T(8,128)(2,1)}) custom-call(s32[9]{0:T(128)} %copy-done.46, bf16[512,1024]{1,0:T(8,128)(2,1)} %bitcast.227, bf16[512,1024]{1,0:T(8,128)(2,1)} %copy-done.52, bf16[512,1024]{1,0:T(8,128)(2,1)} %collective-permute-done.1.x2, ...), custom_call_target="tpu_custom_call" | custom-call | flops 5737807872 | bytes 8388608 | tf_op jit(solution)/shard_map/project_qkv/pallas_call | solution.py:88
  205.4 31.2 %mixer_forward.1 = (bf16[2048,256]{1,0:T(8,128)(2,1)}, f32[2048,256]{1,0:T(8,128)}, f32[8,8,256]{2,1,0:T(8,128)}, bf16[32,2,128,128]{3,2,1,0:T(8,128)(2,1)}) custom-call(s32[9]{0:T(128)} %copy-done.46, f32[4]{0:T(128)} %pad_maximum_fusion.19.fmeta, bf16[3,2048,256]{2,1,0:T(8,128)(2,1)} %get-tuple-element.102.qkv), custom_call_target="tpu_custom_call" | custom-call | flops 4000000000 | bytes 12000000 | tf_op jit(solution)/shard_map/mixer_forward/pallas_call | solution.py:216
  237.8 2.5 collective-permute-start.21
  244.7 2.9 collective-permute-done.21
  248.4 4.4 out_forward.3
  252.8 5.5 all-to-all-start.1
  258.8 4.3 out_forward.2
  268.5 15.6 %all-to-all-done.1 = bf16[8,64,1024]{2,1,0:T(8,128)(2,1)} async-done(((bf16[8,64,1024]{2,1,0:T(8,128)(2,1)}), bf16[8,64,1024]{2,1,0:T(8,128)(2,1)}, u32[]{:S(2)}, u32[]{:S(2)}) %all-to-all-start.1) | async-done | bytes 1048608 | tf_op jit(solution)/shard_map/all_to_all | solution.py:799
  286.7 6.1 collective-permute-done.39.x0
  292.8 21.7 %collective-permute-done.41.g0 = bf16[512,1024]{1,0:T(8,128)(2,1)} collective-permute-done((bf16[512,1024]{1,0:T(8,128)(2,1)}, bf16[512,1024]{1,0:T(8,128)(2,1)}, u32[]{:S(2)}, u32[]{:S(2)}) %collective-permute-start.41) | collective-permute-done | bytes 1048608 | tf_op jit(solution)/shard_map/ppermute | solution.py:762
  322.4 3.1 pad_maximum_fusion.refs_5_
  325.5 3.1 pad_maximum_fusion.1.refs_9_
  328.6 6.5 copy.142
  335.1 22.1 %ffn.3 = (bf16[512,1024]{1,0:T(8,128)(2,1)}, bf16[512,1024]{1,0:T(8,128)(2,1)}, bf16[1024,704]{1,0:T(8,128)(2,1)}, bf16[1024,704]{1,0:T(8,128)(2,1)}, bf16[1024,...) custom-call(s32[9]{0:T(128)} %copy-done.46, ...), custom_call_target="tpu_custom_call" | custom-call | flops 8858370048 | bytes 14000000 | tf_op jit(solution)/shard_map/ffn/pallas_call | solution.py:555
  357.8 22.1 %ffn.2 = (bf16[512,1024]{1,0:T(8,128)(2,1)}, bf16[512,1024]{1,0:T(8,128)(2,1)}, bf16[1024,704]{1,0:T(8,128)(2,1)}, bf16[1024,704]{1,0:T(8,128)(2,1)}, bf16[1024,...) custom-call(s32[9]{0:T(128)} %copy-done.46, ...), custom_call_target="tpu_custom_call" | custom-call | flops 8858370048 | bytes 14000000 | tf_op jit(solution)/shard_map/ffn/pallas_call | solution.py:555
  379.9 7.0 %down.3 = (bf16[1024,1024]{1,0:T(8,128)(2,1)}, bf16[1024,128]{1,0:T(8,128)(2,1)}) custom-call(s32[9]{0:T(128)} %copy-done.46, bf16[1024,704]{1,0:T(8,128)(2,1)} %get-tuple-element.109.refs_0_.refs_8_, bf16[3,1024,704]{2,1,0:T(8,128)(2,1)} %bitcast.246, bf16[704,128]{1,0:T(8,128)(2,1)} %bitcast.304, bf16[1024,128]{1,0:T(8,128)(2,1)} %bitcast.294), custom_call_target="tpu_custom_call" | custom-call | flops 1919313536 | bytes 8000000 | tf_op jit(solution)/shard_map/down/pallas_call | solution.py:600
  389.1 7.2 %down.2 = (bf16[1024,1024]{1,0:T(8,128)(2,1)}, bf16[1024,128]{1,0:T(8,128)(2,1)}) custom-call(s32[9]{0:T(128)} %copy-done.46, bf16[1024,704]{1,0:T(8,128)(2,1)} %get-tuple-element.107.refs_0_.refs_8_, bf16[3,1024,704]{2,1,0:T(8,128)(2,1)} %bitcast.247, bf16[704,128]{1,0:T(8,128)(2,1)} %bitcast.305, bf16[1024,128]{1,0:T(8,128)(2,1)} %bitcast.295), custom_call_target="tpu_custom_call" | custom-call | flops 1919313536 | bytes 8000000 | tf_op jit(solution)/shard_map/down/pallas_call | solution.py:600
  396.4 2.4 slice.184
  403.3 8.2 %pair_sums.3 = (bf16[1024,256]{1,0:T(8,128)(2,1)}, bf16[704,128]{1,0:T(8,128)(2,1)}, bf16[704,128]{1,0:T(8,128)(2,1)}, bf16[704,128]{1,0:T(8,128)(2,1)}, bf16[1024,128]{1,0:T(8,128)(2,1)}) custom-call(bf16[1024,256]{1,0:T(8,128)(2,1)} %get-tuple-element.126.refs_0_, bf16[1024,128]{1,0:T(8,128)(2,1)} %get-tuple-element.170.refs_1_, ...), custom_call_target="tpu_custom_call" | custom-call | flops 2717908992 | bytes 10000000 | tf_op jit(solution)/shard_map/pair_sums/pallas_call | solution.py:652
  411.4 3.2 pad_maximum_fusion.2.refs_5_
  416.6 3.1 pad_maximum_fusion.3.refs_9_
  420.6 7.1 %collective-permute-done.47 = bf16[512,1024]{1,0:T(8,128)(2,1)S(1)} collective-permute-done((bf16[512,1024]{1,0:T(8,128)(2,1)}, bf16[512,1024]{1,0:T(8,128)(2,1)S(1)}, u32[]{:S(2)}, u32[]{:S(2)}) %collective-permute-start.47) | collective-permute-done | bytes 1048608 | tf_op jit(solution)/shard_map/ppermute | solution.py:762
  428.7 21.1 %collective-permute-done.44 = bf16[512,1024]{1,0:T(8,128)(2,1)S(1)} collective-permute-done((bf16[512,1024]{1,0:T(8,128)(2,1)S(1)}, bf16[512,1024]{1,0:T(8,128)(2,1)S(1)}, u32[]{:S(2)}, u32[]{:S(2)}) %collective-permute-start.44) | collective-permute-done | bytes 1048608 | tf_op jit(solution)/shard_map/ppermute | solution.py:762
  449.7 4.9 fusion.17
  454.7 8.2 %pair_sums.4 = (bf16[1024,256]{1,0:T(8,128)(2,1)}, bf16[704,128]{1,0:T(8,128)(2,1)}, bf16[704,128]{1,0:T(8,128)(2,1)}, bf16[704,128]{1,0:T(8,128)(2,1)}, bf16[1024,128]{1,0:T(8,128)(2,1)}) custom-call(bf16[1024,256]{1,0:T(8,128)(2,1)} %get-tuple-element.133.refs_0_, bf16[1024,128]{1,0:T(8,128)(2,1)} %get-tuple-element.172.refs_1_, ...), custom_call_target="tpu_custom_call" | custom-call | flops 2717908992 | bytes 10000000 | tf_op jit(solution)/shard_map/pair_sums/pallas_call | solution.py:652
  466.1 4.3 out_backward.2
  471.3 4.3 out_backward.3
  477.2 3.0 pad_maximum_fusion.4.refs_3_
  480.3 3.8 pair_sums.5
  488.9 6.4 all-to-all-start.2
  499.5 5.2 collective-permute-done.50
  507.0 34.2 %mixer_backward.1.refs_0_.grads = bf16[3,2048,256]{2,1,0:T(8,128)(2,1)} custom-call(s32[9]{0:T(128)} %copy-done.46, f32[4]{0:T(128)} %pad_maximum_fusion.19.fmeta, bf16[3,2048,256]{2,1,0:T(8,128)(2,1)} %get-tuple-element.102.qkv, bf16[4,512,256]{2,1,0:T(8,128)(2,1)} %pad_maximum_fusion.5.grad_out, f32[2048,256]{1,0:T(8,128)} %get-tuple-element.119.attended, ...), custom_call_target="tpu_custom_call" | custom-call | flops 10000000000 | bytes 16000000 | tf_op jit(solution)/shard_map/mixer_backward/pallas_call | solution.py:375
  541.1 5.3 qkv_backward.5
  546.4 8.8 %qkv_pairs.1 = (bf16[1024,384]{1,0:T(8,128)(2,1)}, bf16[3,256,128]{2,1,0:T(8,128)(2,1)}) custom-call(s32[9]{0:T(128)} %copy-done.46, bf16[2048,1024]{1,0:T(8,128)(2,1)} %get-tuple-element.122.normed, bf16[2048,384]{1,0:T(8,128)(2,1)} %get-tuple-element.123.latent, bf16[3,2048,256]{2,1,0:T(8,128)(2,1)} %mixer_backward.1.refs_0_.grads, ...), custom_call_target="tpu_custom_call" | custom-call | flops 3221225472 | bytes 10000000 | tf_op jit(solution)/shard_map/qkv_pairs/pallas_call | solution.py:733
  556.4 5.3 qkv_backward.6
  561.6 5.5 qkv_backward.7
  576.3 6.0 all-to-all-start.4
  582.3 3.0 add_convert_fusion
  592.8 4.7 all-to-all-start.5
  597.9 5.3 qkv_backward.4
  603.2 6.2 collective-permute-done.53
  611.6 3.0 fusion.3
  614.6 3.3 all-to-all-done.5
  617.9 4.3 all-to-all-start.3
  624.8 25.0 %collective-permute-done.57 = f32[96,128]{1,0:T(8,128)S(1)} collective-permute-done((f32[96,128]{1,0:T(8,128)S(1)}, f32[96,128]{1,0:T(8,128)S(1)}, u32[]{:S(2)}, u32[]{:S(2)}) %collective-permute-start.57) | collective-permute-done | bytes 49184 | tf_op jit(solution)/shard_map/ppermute | solution.py:1040
  654.2 7.7 %collective-permute-done.62 = f32[296,128]{1,0:T(8,128)S(1)} collective-permute-done((f32[296,128]{1,0:T(8,128)S(1)}, f32[296,128]{1,0:T(8,128)S(1)}, u32[]{:S(2)}, u32[]{:S(2)}) %collective-permute-start.62) | collective-permute-done | bytes 151584 | tf_op jit(solution)/shard_map/ppermute | solution.py:1040
  (369 shorter events, 148.9 us)
Async XLA Ops:
  7.2 233.2 %all-gather.5.cloned.1.call-start = ((), (), s32[]{:S(2)}) async-start(), calls=%async_computation.6 | async-start | bytes 1935360 | tf_op jit(solution)/shard_map/all_gather | solution.py:936
  9.6 7.7 %collective-permute-start.30 = (bf16[128,128]{1,0:T(8,128)(2,1)S(1)}, bf16[128,128]{1,0:T(8,128)(2,1)S(1)}, u32[]{:S(2)}, u32[]{:S(2)}) collective-permute-start(bf16[128,128]{1,0:T(8,128)(2,1)S(1)} %get-tuple-element.192), channel_id=1, source_target_pairs={{0,1},{1,0},{2,3},{3,2},{4,5},{5,4},{6,7},{7,6},{8,9},{9,8},{10,11... | collective-permute-start | bytes 98312 | tf_op jit(solution)/shard_map/ppermute | solution.py:762
  19.5 7.0 %collective-permute-start.34 = (bf16[32,128]{1,0:T(8,128)(2,1)S(1)}, bf16[32,128]{1,0:T(8,128)(2,1)S(1)}, u32[]{:S(2)}, u32[]{:S(2)}) collective-permute-start(bf16[32,128]{1,0:T(8,128)(2,1)S(1)} %slice.216), channel_id=1, source_target_pairs={{0,2},{1,3},{2,0},{3,1},{4,6},{5,7},{6,4},{7,5},{8,10},{9,11},{10,... | collective-permute-start | bytes 24584 | tf_op jit(solution)/shard_map/ppermute | solution.py:762
  27.2 18.0 %collective-permute-start.11 = (bf16[3,32,128]{2,1,0:T(8,128)(2,1)S(1)}, bf16[3,32,128]{2,1,0:T(8,128)(2,1)S(1)}, u32[]{:S(2)}, u32[]{:S(2)}) collective-permute-start(bf16[3,32,128]{2,1,0:T(8,128)(2,1)S(1)} %copy-done.42), channel_id=1, source_target_pairs={{0,2},{1,3},{2,0},{3,1},{4,6},{5,7},{6,4},{7,5},{8,10},{9,11},{10,... | collective-permute-start | bytes 73736 | tf_op jit(solution)/shard_map/ppermute | solution.py:762
  29.3 18.7 %collective-permute-start.10 = (bf16[3,32,128]{2,1,0:T(8,128)(2,1)S(1)}, bf16[3,32,128]{2,1,0:T(8,128)(2,1)S(1)}, u32[]{:S(2)}, u32[]{:S(2)}) collective-permute-start(bf16[3,32,128]{2,1,0:T(8,128)(2,1)S(1)} %copy-done.42), channel_id=1, source_target_pairs={{0,1},{1,0},{2,3},{3,2},{4,5},{5,4},{6,7},{7,6},{8,9},{9,8},{10,11... | collective-permute-start | bytes 73736 | tf_op jit(solution)/shard_map/ppermute | solution.py:762
  29.3 18.8 %collective-permute-start.13 = (bf16[3,32,128]{2,1,0:T(8,128)(2,1)S(1)}, bf16[3,32,128]{2,1,0:T(8,128)(2,1)S(1)}, u32[]{:S(2)}, u32[]{:S(2)}) collective-permute-start(bf16[3,32,128]{2,1,0:T(8,128)(2,1)S(1)} %bitcast.339), channel_id=1, source_target_pairs={{0,0},{1,4},{2,8},{3,12},{4,16},{5,20},{6,24},{7,28},{8,1},{9,5},{... | collective-permute-start | bytes 73736 | tf_op jit(solution)/shard_map/ppermute | solution.py:895
  31.2 74.8 %collective-permute-start.3 = (bf16[3,128,256]{2,1,0:T(8,128)(2,1)}, bf16[3,128,256]{2,1,0:T(8,128)(2,1)S(1)}, u32[]{:S(2)}, u32[]{:S(2)}) collective-permute-start(bf16[3,128,256]{2,1,0:T(8,128)(2,1)} %param.34), channel_id=1, source_target_pairs={{0,4},{4,0},{8,12},{12,8},{16,20},{20,16},{24,28},{28,24},{1,5},{5... | collective-permute-start | bytes 589832 | tf_op jit(solution)/shard_map/ppermute | solution.py:767
  31.3 115.5 %all-to-all-start = ((bf16[8,64,1024]{2,1,0:T(8,128)(2,1)}), bf16[8,64,1024]{2,1,0:T(8,128)(2,1)S(1)}, u32[]{:S(2)}, u32[]{:S(2)}) async-start(bf16[8,64,1024]{2,1,0:T(8,128)(2,1)} %bitcast), calls=%async_computation | async-start | bytes 2097152 | tf_op jit(solution)/shard_map/all_to_all | solution.py:799
  38.4 290.2 %all-gather.7.cloned.1.call-start = ((), (), s32[]{:S(2)}) async-start(), calls=%async_computation.7 | async-start | bytes 4866048 | tf_op jit(solution)/shard_map/all_gather | solution.py:910
  38.4 14.1 %collective-permute-start.22 = (bf16[128,256]{0,1:T(8,128)(2,1)S(1)}, bf16[128,256]{0,1:T(8,128)(2,1)S(1)}, u32[]{:S(2)}, u32[]{:S(2)}) collective-permute-start(bf16[128,256]{0,1:T(8,128)(2,1)S(1)} %bitcast.329), channel_id=1, source_target_pairs={{0,2},{1,3},{2,0},{3,1},{4,6},{5,7},{6,4},{7,5},{8,10},{9,11},{10,... | collective-permute-start | bytes 196616 | tf_op jit(solution)/shard_map/ppermute | solution.py:762
  48.7 8.3 %collective-permute-start.14 = (bf16[480,128]{1,0:T(8,128)(2,1)}, bf16[480,128]{1,0:T(8,128)(2,1)}, u32[]{:S(2)}, u32[]{:S(2)}) collective-permute-start(bf16[480,128]{1,0:T(8,128)(2,1)} %pad_maximum_fusion.14), channel_id=1, source_target_pairs={{0,4},{4,0},{8,12},{12,8},{16,20},{20,16},{24,28},{28,24},{1,5},{5... | collective-permute-start | bytes 368648 | tf_op jit(solution)/shard_map/ppermute | solution.py:767
  48.9 17.5 %collective-permute-start.15 = (bf16[480,128]{1,0:T(8,128)(2,1)}, bf16[480,128]{1,0:T(8,128)(2,1)S(1)}, u32[]{:S(2)}, u32[]{:S(2)}) collective-permute-start(bf16[480,128]{1,0:T(8,128)(2,1)} %pad_maximum_fusion.14), channel_id=1, source_target_pairs={{0,8},{4,12},{8,0},{12,4},{16,24},{20,28},{24,16},{28,20},{1,9},{5... | collective-permute-start | bytes 368648 | tf_op jit(solution)/shard_map/ppermute | solution.py:767
  53.2 15.8 %collective-permute-start.23 = (bf16[128,512]{0,1:T(8,128)(2,1)}, bf16[128,512]{0,1:T(8,128)(2,1)S(1)}, u32[]{:S(2)}, u32[]{:S(2)}) collective-permute-start(bf16[128,512]{0,1:T(8,128)(2,1)} %get-tuple-element.187), channel_id=1, source_target_pairs={{0,4},{4,0},{8,12},{12,8},{16,20},{20,16},{24,28},{28,24},{1,5},{5... | collective-permute-start | bytes 393224 | tf_op jit(solution)/shard_map/ppermute | solution.py:767
  54.7 17.3 %collective-permute-start.24 = (bf16[128,512]{0,1:T(8,128)(2,1)}, bf16[128,512]{0,1:T(8,128)(2,1)S(1)}, u32[]{:S(2)}, u32[]{:S(2)}) collective-permute-start(bf16[128,512]{0,1:T(8,128)(2,1)} %get-tuple-element.187), channel_id=1, source_target_pairs={{0,8},{4,12},{8,0},{12,4},{16,24},{20,28},{24,16},{28,20},{1,9},{5... | collective-permute-start | bytes 393224 | tf_op jit(solution)/shard_map/ppermute | solution.py:767
  57.1 34.3 %collective-permute-start.26 = (bf16[128,512]{0,1:T(8,128)(2,1)}, bf16[128,512]{0,1:T(8,128)(2,1)S(1)}, u32[]{:S(2)}, u32[]{:S(2)}) collective-permute-start(bf16[128,512]{0,1:T(8,128)(2,1)} %get-tuple-element.187), channel_id=1, source_target_pairs={{0,16},{4,20},{8,24},{12,28},{16,0},{20,4},{24,8},{28,12},{1,17},{... | collective-permute-start | bytes 393224 | tf_op jit(solution)/shard_map/ppermute | solution.py:767
  66.3 26.0 %collective-permute-start.28 = (bf16[128,512]{0,1:T(8,128)(2,1)}, bf16[128,512]{0,1:T(8,128)(2,1)}, u32[]{:S(2)}, u32[]{:S(2)}) collective-permute-start(bf16[128,512]{0,1:T(8,128)(2,1)} %get-tuple-element.187), channel_id=1, source_target_pairs={{0,24},{4,28},{8,16},{12,20},{16,8},{20,12},{24,0},{28,4},{1,25},{... | collective-permute-start | bytes 393224 | tf_op jit(solution)/shard_map/ppermute | solution.py:767
  69.0 69.3 %collective-permute-start.4 = (bf16[3,128,256]{2,1,0:T(8,128)(2,1)}, bf16[3,128,256]{2,1,0:T(8,128)(2,1)}, u32[]{:S(2)}, u32[]{:S(2)}) collective-permute-start(bf16[3,128,256]{2,1,0:T(8,128)(2,1)} %param.34), channel_id=1, source_target_pairs={{0,8},{4,12},{8,0},{12,4},{16,24},{20,28},{24,16},{28,20},{1,9},{5... | collective-permute-start | bytes 589832 | tf_op jit(solution)/shard_map/ppermute | solution.py:767
  72.0 91.6 %collective-permute-start.6 = (bf16[3,128,256]{2,1,0:T(8,128)(2,1)}, bf16[3,128,256]{2,1,0:T(8,128)(2,1)}, u32[]{:S(2)}, u32[]{:S(2)}) collective-permute-start(bf16[3,128,256]{2,1,0:T(8,128)(2,1)} %param.34), channel_id=1, source_target_pairs={{0,16},{4,20},{8,24},{12,28},{16,0},{20,4},{24,8},{28,12},{1,17},{... | collective-permute-start | bytes 589832 | tf_op jit(solution)/shard_map/ppermute | solution.py:767
  91.4 74.1 %collective-permute-start.8 = (bf16[3,128,256]{2,1,0:T(8,128)(2,1)}, bf16[3,128,256]{2,1,0:T(8,128)(2,1)S(1)}, u32[]{:S(2)}, u32[]{:S(2)}) collective-permute-start(bf16[3,128,256]{2,1,0:T(8,128)(2,1)} %param.34), channel_id=1, source_target_pairs={{0,24},{4,28},{8,16},{12,20},{16,8},{20,12},{24,0},{28,4},{1,25},{... | collective-permute-start | bytes 589832 | tf_op jit(solution)/shard_map/ppermute | solution.py:767
  92.3 43.9 %collective-permute-start.17 = (bf16[480,128]{1,0:T(8,128)(2,1)}, bf16[480,128]{1,0:T(8,128)(2,1)}, u32[]{:S(2)}, u32[]{:S(2)}) collective-permute-start(bf16[480,128]{1,0:T(8,128)(2,1)} %pad_maximum_fusion.14), channel_id=1, source_target_pairs={{0,16},{4,20},{8,24},{12,28},{16,0},{20,4},{24,8},{28,12},{1,17},{... | collective-permute-start | bytes 368648 | tf_op jit(solution)/shard_map/ppermute | solution.py:767
  106.0 30.8 %collective-permute-start.19 = (bf16[480,128]{1,0:T(8,128)(2,1)}, bf16[480,128]{1,0:T(8,128)(2,1)S(1)}, u32[]{:S(2)}, u32[]{:S(2)}) collective-permute-start(bf16[480,128]{1,0:T(8,128)(2,1)} %pad_maximum_fusion.14), channel_id=1, source_target_pairs={{0,24},{4,28},{8,16},{12,20},{16,8},{20,12},{24,0},{28,4},{1,25},{... | collective-permute-start | bytes 368648 | tf_op jit(solution)/shard_map/ppermute | solution.py:767
  136.8 9.9 %collective-permute-start.18 = (bf16[480,128]{1,0:T(8,128)(2,1)}, bf16[480,128]{1,0:T(8,128)(2,1)}, u32[]{:S(2)}, u32[]{:S(2)}) collective-permute-start(bf16[480,128]{1,0:T(8,128)(2,1)} %collective-permute-done.17), channel_id=1, source_target_pairs={{0,4},{4,0},{8,12},{12,8},{16,20},{20,16},{24,28},{28,24},{1,5},{5... | collective-permute-start | bytes 368648 | tf_op jit(solution)/shard_map/ppermute | solution.py:767
  138.3 13.7 %collective-permute-start.20 = (bf16[480,128]{1,0:T(8,128)(2,1)S(1)}, bf16[480,128]{1,0:T(8,128)(2,1)S(1)}, u32[]{:S(2)}, u32[]{:S(2)}) collective-permute-start(bf16[480,128]{1,0:T(8,128)(2,1)S(1)} %collective-permute-done.19), channel_id=1, source_target_pairs={{0,4},{4,0},{8,12},{12,8},{16,20},{20,16},{24,28},{28,24},{1,5},{5... | collective-permute-start | bytes 368648 | tf_op jit(solution)/shard_map/ppermute | solution.py:767
  142.7 14.8 %collective-permute-start.25 = (bf16[128,512]{0,1:T(8,128)(2,1)}, bf16[128,512]{0,1:T(8,128)(2,1)S(1)}, u32[]{:S(2)}, u32[]{:S(2)}) collective-permute-start(bf16[128,512]{0,1:T(8,128)(2,1)} %copy-done.36), channel_id=1, source_target_pairs={{0,4},{4,0},{8,12},{12,8},{16,20},{20,16},{24,28},{28,24},{1,5},{5... | collective-permute-start | bytes 393224 | tf_op jit(solution)/shard_map/ppermute | solution.py:767
  146.7 25.8 %collective-permute-start.1 = (bf16[512,1024]{1,0:T(8,128)(2,1)S(1)}, bf16[512,1024]{1,0:T(8,128)(2,1)}, u32[]{:S(2)}, u32[]{:S(2)}) collective-permute-start(bf16[512,1024]{1,0:T(8,128)(2,1)S(1)} %bitcast.225), channel_id=1, source_target_pairs={{0,2},{1,3},{2,0},{3,1},{4,6},{5,7},{6,4},{7,5},{8,10},{9,11},{10,... | collective-permute-start | bytes 3145736 | tf_op jit(solution)/shard_map/ppermute | solution.py:762
  151.9 13.7 %collective-permute-start.27 = (bf16[128,512]{0,1:T(8,128)(2,1)}, bf16[128,512]{0,1:T(8,128)(2,1)}, u32[]{:S(2)}, u32[]{:S(2)}) collective-permute-start(bf16[128,512]{0,1:T(8,128)(2,1)} %copy-done.35), channel_id=1, source_target_pairs={{0,4},{4,0},{8,12},{12,8},{16,20},{20,16},{24,28},{28,24},{1,5},{5... | collective-permute-start | bytes 393224 | tf_op jit(solution)/shard_map/ppermute | solution.py:767
  157.5 11.3 %collective-permute-start.29 = (bf16[128,512]{0,1:T(8,128)(2,1)}, bf16[128,512]{0,1:T(8,128)(2,1)}, u32[]{:S(2)}, u32[]{:S(2)}) collective-permute-start(bf16[128,512]{0,1:T(8,128)(2,1)} %collective-permute-done.28), channel_id=1, source_target_pairs={{0,4},{4,0},{8,12},{12,8},{16,20},{20,16},{24,28},{28,24},{1,5},{5... | collective-permute-start | bytes 393224 | tf_op jit(solution)/shard_map/ppermute | solution.py:767
  163.5 13.8 %collective-permute-start.5 = (bf16[3,128,256]{2,1,0:T(8,128)(2,1)}, bf16[3,128,256]{2,1,0:T(8,128)(2,1)}, u32[]{:S(2)}, u32[]{:S(2)}) collective-permute-start(bf16[3,128,256]{2,1,0:T(8,128)(2,1)} %collective-permute-done.4), channel_id=1, source_target_pairs={{0,4},{4,0},{8,12},{12,8},{16,20},{20,16},{24,28},{28,24},{1,5},{5... | collective-permute-start | bytes 589832 | tf_op jit(solution)/shard_map/ppermute | solution.py:767
  165.6 19.7 %collective-permute-start.7 = (bf16[3,128,256]{2,1,0:T(8,128)(2,1)}, bf16[3,128,256]{2,1,0:T(8,128)(2,1)}, u32[]{:S(2)}, u32[]{:S(2)}) collective-permute-start(bf16[3,128,256]{2,1,0:T(8,128)(2,1)} %collective-permute-done.6), channel_id=1, source_target_pairs={{0,4},{4,0},{8,12},{12,8},{16,20},{20,16},{24,28},{28,24},{1,5},{5... | collective-permute-start | bytes 589832 | tf_op jit(solution)/shard_map/ppermute | solution.py:767
  165.6 24.0 %collective-permute-start.9 = (bf16[3,128,256]{2,1,0:T(8,128)(2,1)S(1)}, bf16[3,128,256]{2,1,0:T(8,128)(2,1)S(1)}, u32[]{:S(2)}, u32[]{:S(2)}) collective-permute-start(bf16[3,128,256]{2,1,0:T(8,128)(2,1)S(1)} %collective-permute-done.8), channel_id=1, source_target_pairs={{0,4},{4,0},{8,12},{12,8},{16,20},{20,16},{24,28},{28,24},{1,5},{5... | collective-permute-start | bytes 589832 | tf_op jit(solution)/shard_map/ppermute | solution.py:767
  172.5 17.1 %collective-permute-start = (bf16[512,1024]{1,0:T(8,128)(2,1)S(1)}, bf16[512,1024]{1,0:T(8,128)(2,1)S(1)}, u32[]{:S(2)}, u32[]{:S(2)}) collective-permute-start(bf16[512,1024]{1,0:T(8,128)(2,1)S(1)} %bitcast.226), channel_id=1, source_target_pairs={{0,1},{1,0},{2,3},{3,2},{4,5},{5,4},{6,7},{7,6},{8,9},{9,8},{10,11... | collective-permute-start | bytes 3145736 | tf_op jit(solution)/shard_map/ppermute | solution.py:762
  172.5 17.1 %collective-permute-start.2 = (bf16[512,1024]{1,0:T(8,128)(2,1)}, bf16[512,1024]{1,0:T(8,128)(2,1)S(1)}, u32[]{:S(2)}, u32[]{:S(2)}) collective-permute-start(bf16[512,1024]{1,0:T(8,128)(2,1)} %collective-permute-done.1.x2), channel_id=1, source_target_pairs={{0,1},{1,0},{2,3},{3,2},{4,5},{5,4},{6,7},{7,6},{8,9},{9,8},{10,11... | collective-permute-start | bytes 3145736 | tf_op jit(solution)/shard_map/ppermute | solution.py:762
  237.8 9.7 %collective-permute-start.21 = (bf16[1024,256]{1,0:T(8,128)(2,1)S(1)}, bf16[1024,256]{1,0:T(8,128)(2,1)S(1)}, u32[]{:S(2)}, u32[]{:S(2)}) collective-permute-start(bf16[1024,256]{1,0:T(8,128)(2,1)S(1)} %constant_dynamic-slice_fusion.3), channel_id=1, source_target_pairs={{0,2},{1,3},{2,0},{3,1},{4,6},{5,7},{6,4},{7,5},{8,10},{9,11},{10,... | collective-permute-start | bytes 1572872 | tf_op jit(solution)/shard_map/ppermute | solution.py:762
  252.8 10.3 %collective-permute-start.35 = (bf16[512,1024]{1,0:T(8,128)(2,1)}, bf16[512,1024]{1,0:T(8,128)(2,1)S(1)}, u32[]{:S(2)}, u32[]{:S(2)}) collective-permute-start(bf16[512,1024]{1,0:T(8,128)(2,1)} %get-tuple-element.105), channel_id=1, source_target_pairs={{0,1},{1,0},{2,3},{3,2},{4,5},{5,4},{6,7},{7,6},{8,9},{9,8},{10,11... | collective-permute-start | bytes 3145736 | tf_op jit(solution)/shard_map/ppermute | solution.py:762
  252.8 31.4 %all-to-all-start.1 = ((bf16[8,64,1024]{2,1,0:T(8,128)(2,1)}), bf16[8,64,1024]{2,1,0:T(8,128)(2,1)}, u32[]{:S(2)}, u32[]{:S(2)}) async-start(bf16[8,64,1024]{2,1,0:T(8,128)(2,1)} %bitcast.80), calls=%async_computation.1 | async-start | bytes 2097152 | tf_op jit(solution)/shard_map/all_to_all | solution.py:799
  266.5 26.3 %collective-permute-start.39 = (bf16[512,1024]{1,0:T(8,128)(2,1)}, bf16[512,1024]{1,0:T(8,128)(2,1)}, u32[]{:S(2)}, u32[]{:S(2)}) collective-permute-start(bf16[512,1024]{1,0:T(8,128)(2,1)} %multiply_convert_fusion.x0), channel_id=1, source_target_pairs={{0,2},{1,3},{2,0},{3,1},{4,6},{5,7},{6,4},{7,5},{8,10},{9,11},{10,... | collective-permute-start | bytes 3145736 | tf_op jit(solution)/shard_map/ppermute | solution.py:762
  284.1 30.4 %collective-permute-start.41 = (bf16[512,1024]{1,0:T(8,128)(2,1)}, bf16[512,1024]{1,0:T(8,128)(2,1)}, u32[]{:S(2)}, u32[]{:S(2)}) collective-permute-start(bf16[512,1024]{1,0:T(8,128)(2,1)} %bitcast.81.g0), channel_id=1, source_target_pairs={{0,2},{1,3},{2,0},{3,1},{4,6},{5,7},{6,4},{7,5},{8,10},{9,11},{10,... | collective-permute-start | bytes 3145736 | tf_op jit(solution)/shard_map/ppermute | solution.py:762
  286.2 36.3 %collective-permute-start.36 = (bf16[512,1024]{1,0:T(8,128)(2,1)}, bf16[512,1024]{1,0:T(8,128)(2,1)}, u32[]{:S(2)}, u32[]{:S(2)}) collective-permute-start(bf16[512,1024]{1,0:T(8,128)(2,1)} %multiply_convert_fusion.x0), channel_id=1, source_target_pairs={{0,1},{1,0},{2,3},{3,2},{4,5},{5,4},{6,7},{7,6},{8,9},{9,8},{10,11... | collective-permute-start | bytes 3145736 | tf_op jit(solution)/shard_map/ppermute | solution.py:762
  286.2 39.3 %collective-permute-start.37 = (bf16[512,1024]{1,0:T(8,128)(2,1)}, bf16[512,1024]{1,0:T(8,128)(2,1)}, u32[]{:S(2)}, u32[]{:S(2)}) collective-permute-start(bf16[512,1024]{1,0:T(8,128)(2,1)} %bitcast.81.g0), channel_id=1, source_target_pairs={{0,1},{1,0},{2,3},{3,2},{4,5},{5,4},{6,7},{7,6},{8,9},{9,8},{10,11... | collective-permute-start | bytes 3145736 | tf_op jit(solution)/shard_map/ppermute | solution.py:762
  292.8 42.4 %collective-permute-start.40 = (bf16[512,1024]{1,0:T(8,128)(2,1)}, bf16[512,1024]{1,0:T(8,128)(2,1)}, u32[]{:S(2)}, u32[]{:S(2)}) collective-permute-start(bf16[512,1024]{1,0:T(8,128)(2,1)} %collective-permute-done.39.x0), channel_id=1, source_target_pairs={{0,1},{1,0},{2,3},{3,2},{4,5},{5,4},{6,7},{7,6},{8,9},{9,8},{10,11... | collective-permute-start | bytes 3145736 | tf_op jit(solution)/shard_map/ppermute | solution.py:762
  314.5 20.6 %collective-permute-start.42 = (bf16[512,1024]{1,0:T(8,128)(2,1)}, bf16[512,1024]{1,0:T(8,128)(2,1)}, u32[]{:S(2)}, u32[]{:S(2)}) collective-permute-start(bf16[512,1024]{1,0:T(8,128)(2,1)} %collective-permute-done.41.g0), channel_id=1, source_target_pairs={{0,1},{1,0},{2,3},{3,2},{4,5},{5,4},{6,7},{7,6},{8,9},{9,8},{10,11... | collective-permute-start | bytes 3145736 | tf_op jit(solution)/shard_map/ppermute | solution.py:762
  357.2 42.9 %collective-permute-start.46 = (bf16[512,1024]{1,0:T(8,128)(2,1)}, bf16[512,1024]{1,0:T(8,128)(2,1)S(1)}, u32[]{:S(2)}, u32[]{:S(2)}) collective-permute-start(bf16[512,1024]{1,0:T(8,128)(2,1)} %get-tuple-element.114), channel_id=1, source_target_pairs={{0,1},{1,0},{2,3},{3,2},{4,5},{5,4},{6,7},{7,6},{8,9},{9,8},{10,11... | collective-permute-start | bytes 3145736 | tf_op jit(solution)/shard_map/ppermute | solution.py:762
  389.1 25.5 %collective-permute-start.43 = (bf16[512,1024]{1,0:T(8,128)(2,1)}, bf16[512,1024]{1,0:T(8,128)(2,1)}, u32[]{:S(2)}, u32[]{:S(2)}) collective-permute-start(bf16[512,1024]{1,0:T(8,128)(2,1)} %slice.186), channel_id=1, source_target_pairs={{0,1},{1,0},{2,3},{3,2},{4,5},{5,4},{6,7},{7,6},{8,9},{9,8},{10,11... | collective-permute-start | bytes 3145736 | tf_op jit(solution)/shard_map/ppermute | solution.py:762
  398.8 29.9 %collective-permute-start.38 = (bf16[512,1024]{1,0:T(8,128)(2,1)}, bf16[512,1024]{1,0:T(8,128)(2,1)}, u32[]{:S(2)}, u32[]{:S(2)}) collective-permute-start(bf16[512,1024]{1,0:T(8,128)(2,1)} %slice.184), channel_id=1, source_target_pairs={{0,1},{1,0},{2,3},{3,2},{4,5},{5,4},{6,7},{7,6},{8,9},{9,8},{10,11... | collective-permute-start | bytes 3145736 | tf_op jit(solution)/shard_map/ppermute | solution.py:762
  399.3 21.3 %collective-permute-start.45 = (bf16[512,1024]{1,0:T(8,128)(2,1)}, bf16[512,1024]{1,0:T(8,128)(2,1)S(1)}, u32[]{:S(2)}, u32[]{:S(2)}) collective-permute-start(bf16[512,1024]{1,0:T(8,128)(2,1)} %get-tuple-element.112), channel_id=1, source_target_pairs={{0,1},{1,0},{2,3},{3,2},{4,5},{5,4},{6,7},{7,6},{8,9},{9,8},{10,11... | collective-permute-start | bytes 3145736 | tf_op jit(solution)/shard_map/ppermute | solution.py:762
  401.5 26.2 %collective-permute-start.47 = (bf16[512,1024]{1,0:T(8,128)(2,1)}, bf16[512,1024]{1,0:T(8,128)(2,1)S(1)}, u32[]{:S(2)}, u32[]{:S(2)}) collective-permute-start(bf16[512,1024]{1,0:T(8,128)(2,1)} %add_convert_fusion.1), channel_id=1, source_target_pairs={{0,2},{1,3},{2,0},{3,1},{4,6},{5,7},{6,4},{7,5},{8,10},{9,11},{10,... | collective-permute-start | bytes 3145736 | tf_op jit(solution)/shard_map/ppermute | solution.py:762
  416.3 33.5 %collective-permute-start.44 = (bf16[512,1024]{1,0:T(8,128)(2,1)S(1)}, bf16[512,1024]{1,0:T(8,128)(2,1)S(1)}, u32[]{:S(2)}, u32[]{:S(2)}) collective-permute-start(bf16[512,1024]{1,0:T(8,128)(2,1)S(1)} %add_convert_fusion.3), channel_id=1, source_target_pairs={{0,2},{1,3},{2,0},{3,1},{4,6},{5,7},{6,4},{7,5},{8,10},{9,11},{10,... | collective-permute-start | bytes 3145736 | tf_op jit(solution)/shard_map/ppermute | solution.py:762
  454.7 15.7 %collective-permute-start.48 = (bf16[512,1024]{1,0:T(8,128)(2,1)}, bf16[512,1024]{1,0:T(8,128)(2,1)S(1)}, u32[]{:S(2)}, u32[]{:S(2)}) collective-permute-start(bf16[512,1024]{1,0:T(8,128)(2,1)} %get-tuple-element.156.grad), channel_id=1, source_target_pairs={{0,1},{1,0},{2,3},{3,2},{4,5},{5,4},{6,7},{7,6},{8,9},{9,8},{10,11... | collective-permute-start | bytes 3145736 | tf_op jit(solution)/shard_map/ppermute | solution.py:762
  485.9 12.2 %collective-permute-start.59 = (bf16[8,32,512]{2,1,0:T(8,128)(2,1)}, bf16[8,32,512]{2,1,0:T(8,128)(2,1)}, u32[]{:S(2)}, u32[]{:S(2)}) collective-permute-start(bf16[8,32,512]{2,1,0:T(8,128)(2,1)} %get-tuple-element.164), channel_id=1, source_target_pairs={{0,1},{1,0},{2,3},{3,2},{4,5},{5,4},{6,7},{7,6},{8,9},{9,8},{10,11... | collective-permute-start | bytes 786440 | tf_op jit(solution)/shard_map/ppermute | solution.py:762
  487.1 12.4 %collective-permute-start.49 = (bf16[512,256]{1,0:T(8,128)(2,1)}, bf16[512,256]{1,0:T(8,128)(2,1)}, u32[]{:S(2)}, u32[]{:S(2)}) collective-permute-start(bf16[512,256]{1,0:T(8,128)(2,1)} %get-tuple-element.117), channel_id=1, source_target_pairs={{0,2},{1,3},{2,0},{3,1},{4,6},{5,7},{6,4},{7,5},{8,10},{9,11},{10,... | collective-permute-start | bytes 786440 | tf_op jit(solution)/shard_map/ppermute | solution.py:762
  488.9 87.4 %all-to-all-start.2 = ((bf16[8,64,1024]{2,1,0:T(8,128)(2,1)}), bf16[8,64,1024]{2,1,0:T(8,128)(2,1)S(1)}, u32[]{:S(2)}, u32[]{:S(2)}) async-start(bf16[8,64,1024]{2,1,0:T(8,128)(2,1)} %bitcast.96), calls=%async_computation.2 | async-start | bytes 2097152 | tf_op jit(solution)/shard_map/all_to_all | solution.py:799
  495.3 72.6 %collective-permute-start.58 = (bf16[8,32,512]{2,1,0:T(8,128)(2,1)S(1)}, bf16[8,32,512]{2,1,0:T(8,128)(2,1)S(1)}, u32[]{:S(2)}, u32[]{:S(2)}) collective-permute-start(bf16[8,32,512]{2,1,0:T(8,128)(2,1)S(1)} %get-tuple-element.163), channel_id=1, source_target_pairs={{0,1},{1,0},{2,3},{3,2},{4,5},{5,4},{6,7},{7,6},{8,9},{9,8},{10,11... | collective-permute-start | bytes 786440 | tf_op jit(solution)/shard_map/ppermute | solution.py:762
  495.4 9.4 %collective-permute-start.50 = (bf16[512,256]{1,0:T(8,128)(2,1)}, bf16[512,256]{1,0:T(8,128)(2,1)S(1)}, u32[]{:S(2)}, u32[]{:S(2)}) collective-permute-start(bf16[512,256]{1,0:T(8,128)(2,1)} %get-tuple-element.118), channel_id=1, source_target_pairs={{0,2},{1,3},{2,0},{3,1},{4,6},{5,7},{6,4},{7,5},{8,10},{9,11},{10,... | collective-permute-start | bytes 786440 | tf_op jit(solution)/shard_map/ppermute | solution.py:762
  496.4 92.7 %collective-permute-start.61 = (bf16[8,32,128]{2,1,0:T(8,128)(2,1)}, bf16[8,32,128]{2,1,0:T(8,128)(2,1)}, u32[]{:S(2)}, u32[]{:S(2)}) collective-permute-start(bf16[8,32,128]{2,1,0:T(8,128)(2,1)} %bitcast.125), channel_id=1, source_target_pairs={{0,2},{1,3},{2,0},{3,1},{4,6},{5,7},{6,4},{7,5},{8,10},{9,11},{10,... | collective-permute-start | bytes 196616 | tf_op jit(solution)/shard_map/ppermute | solution.py:762
  499.2 69.3 %collective-permute-start.60 = (bf16[8,32,512]{2,1,0:T(8,128)(2,1)S(1)}, bf16[8,32,512]{2,1,0:T(8,128)(2,1)S(1)}, u32[]{:S(2)}, u32[]{:S(2)}) collective-permute-start(bf16[8,32,512]{2,1,0:T(8,128)(2,1)S(1)} %fusion.4), channel_id=1, source_target_pairs={{0,2},{1,3},{2,0},{3,1},{4,6},{5,7},{6,4},{7,5},{8,10},{9,11},{10,... | collective-permute-start | bytes 786440 | tf_op jit(solution)/shard_map/ppermute | solution.py:762
  556.3 11.4 %collective-permute-start.55 = (bf16[8,32,384]{2,1,0:T(8,128)(2,1)S(1)}, bf16[8,32,384]{2,1,0:T(8,128)(2,1)S(1)}, u32[]{:S(2)}, u32[]{:S(2)}) collective-permute-start(bf16[8,32,384]{2,1,0:T(8,128)(2,1)S(1)} %get-tuple-element.168), channel_id=1, source_target_pairs={{0,1},{1,0},{2,3},{3,2},{4,5},{5,4},{6,7},{7,6},{8,9},{9,8},{10,11... | collective-permute-start | bytes 589832 | tf_op jit(solution)/shard_map/ppermute | solution.py:762
  567.7 35.4 %collective-permute-start.51 = (bf16[512,1024]{1,0:T(8,128)(2,1)}, bf16[512,1024]{1,0:T(8,128)(2,1)S(1)}, u32[]{:S(2)}, u32[]{:S(2)}) collective-permute-start(bf16[512,1024]{1,0:T(8,128)(2,1)} %qkv_backward.5), channel_id=1, source_target_pairs={{0,1},{1,0},{2,3},{3,2},{4,5},{5,4},{6,7},{7,6},{8,9},{9,8},{10,11... | collective-permute-start | bytes 3145736 | tf_op jit(solution)/shard_map/ppermute | solution.py:762
  567.9 14.4 %collective-permute-start.52 = (bf16[512,1024]{1,0:T(8,128)(2,1)}, bf16[512,1024]{1,0:T(8,128)(2,1)}, u32[]{:S(2)}, u32[]{:S(2)}) collective-permute-start(bf16[512,1024]{1,0:T(8,128)(2,1)} %qkv_backward.7), channel_id=1, source_target_pairs={{0,1},{1,0},{2,3},{3,2},{4,5},{5,4},{6,7},{7,6},{8,9},{9,8},{10,11... | collective-permute-start | bytes 3145736 | tf_op jit(solution)/shard_map/ppermute | solution.py:762
  576.3 16.5 %all-to-all-start.4 = ((bf16[8,192,128]{2,1,0:T(8,128)(2,1)}), bf16[8,192,128]{2,1,0:T(8,128)(2,1)S(1)}, u32[]{:S(2)}, u32[]{:S(2)}) async-start(bf16[8,192,128]{2,1,0:T(8,128)(2,1)} %pad_maximum_fusion.8), calls=%async_computation.4 | async-start | bytes 786432 | tf_op jit(solution)/shard_map/all_to_all | solution.py:799
  585.3 24.1 %collective-permute-start.53 = (bf16[512,1024]{1,0:T(8,128)(2,1)}, bf16[512,1024]{1,0:T(8,128)(2,1)}, u32[]{:S(2)}, u32[]{:S(2)}) collective-permute-start(bf16[512,1024]{1,0:T(8,128)(2,1)} %add_convert_fusion), channel_id=1, source_target_pairs={{0,2},{1,3},{2,0},{3,1},{4,6},{5,7},{6,4},{7,5},{8,10},{9,11},{10,... | collective-permute-start | bytes 3145736 | tf_op jit(solution)/shard_map/ppermute | solution.py:762
  592.8 25.1 %all-to-all-start.5 = ((bf16[8,424,128]{2,1,0:T(8,128)(2,1)}), bf16[8,424,128]{2,1,0:T(8,128)(2,1)}, u32[]{:S(2)}, u32[]{:S(2)}) async-start(bf16[8,424,128]{2,1,0:T(8,128)(2,1)} %fusion.12), calls=%async_computation.5 | async-start | bytes 1736704 | tf_op jit(solution)/shard_map/all_to_all | solution.py:799
  617.9 45.9 %all-to-all-start.3 = ((bf16[8,64,1024]{2,1,0:T(8,128)(2,1)}), bf16[8,64,1024]{2,1,0:T(8,128)(2,1)S(1)}, u32[]{:S(2)}, u32[]{:S(2)}) async-start(bf16[8,64,1024]{2,1,0:T(8,128)(2,1)} %bitcast.255), calls=%async_computation.3 | async-start | bytes 2097152 | tf_op jit(solution)/shard_map/all_to_all | solution.py:799
  622.9 26.9 %collective-permute-start.57 = (f32[96,128]{1,0:T(8,128)S(1)}, f32[96,128]{1,0:T(8,128)S(1)}, u32[]{:S(2)}, u32[]{:S(2)}) collective-permute-start(f32[96,128]{1,0:T(8,128)S(1)} %get-tuple-element.189), channel_id=1, source_target_pairs={{0,0},{4,1},{8,2},{12,3},{16,4},{20,5},{24,6},{28,7},{1,8},{5,9},{... | collective-permute-start | bytes 147464 | tf_op jit(solution)/shard_map/ppermute | solution.py:1040
  651.7 10.2 %collective-permute-start.62 = (f32[296,128]{1,0:T(8,128)S(1)}, f32[296,128]{1,0:T(8,128)S(1)}, u32[]{:S(2)}, u32[]{:S(2)}) collective-permute-start(f32[296,128]{1,0:T(8,128)S(1)} %slice.233), channel_id=1, source_target_pairs={{0,0},{4,1},{8,2},{12,3},{16,4},{20,5},{24,6},{28,7},{1,8},{5,9},{... | collective-permute-start | bytes 454664 | tf_op jit(solution)/shard_map/ppermute | solution.py:1040
  (66 other events, 551.4 us)
Sparse Core Ops, SparseCore 0:
  27.3 65.1 all-gather.4
  94.7 110.0 all-gather.6
